TPU v7x, 256 devices: a whole 4x4x8 slice. The times are simulated.
256 devices in a mesh: gx: 8 (over y, core), gy: 32 (over x, z).
Axes of the slice: x: 4, y: 4, z: 8, core: 2. Of those that a mesh axis runs over, the one named last changes fastest.
Arguments:
- forcing_field: float32 [64, 1024, 1024], P(None, 'gy', 'gx'), may hold values from -6 to 6
- innovations: float32 [524288, 64], P(('gx', 'gy')), may hold values from -6 to 6
- owner_device: int32 [524288, 1], P(('gx', 'gy')), may hold values from 0 to 255; in each aligned block of 2048 rows (0 to 2047, 2048 to 4095, ...) at most 16 rows name the same one
- column_index: int32 [524288], P(('gx', 'gy')), may hold values from 0 to 4095
- obs_weight: float32 [64, 64], replicated, may hold values from -0.75 to 0.75
- vert_inverse: float32 [64, 64], replicated, may hold values from -0.3 to 1.3
- vert_basis: float32 [64, 64], replicated, may hold values from -0.3 to 1.3
- vert_eigen: float32 [64], replicated, may hold values from 0.002 to 2
Outputs:
- pressure_adjoint: float32 [64, 1024, 1024], P(None, 'gy', 'gx')
Inputs may be any that keep to these rules, and one draw needn't show every extreme that they name: `owner_device`: the rows of one device name any one owner at most 16 times.
All inputs are finite; a program needn't handle non-finite values.
Results may differ from a plain program's by a relative error of at most 0.00011.
Values sent between devices are 32-bit elements; how exact they have to be, the bound alone decides.
A program may use at most 64 MiB of HBM per device.

v0:
```python
import jax
import jax.numpy as jnp
from jax import lax
from jax.sharding import PartitionSpec as P


def cosine_table(length):
    frequency = jnp.arange(length, dtype=jnp.float32)[:, None]
    points = jnp.arange(length, dtype=jnp.float32)[None, :]
    scales = jnp.where(frequency == 0, jnp.sqrt(1.0 / length), jnp.sqrt(2.0 / length))
    return scales * jnp.cos(jnp.pi * frequency * (2.0 * points + 1.0) / (2.0 * length))


def eigen_line(wave_ids, length):
    return 4.0 * jnp.sin(jnp.pi * wave_ids / (2.0 * length)) ** 2


def per_device(
    forcing_field,
    innovations,
    owner_device,
    column_index,
    obs_weight,
    vert_inverse,
    vert_basis,
    vert_eigen,
):
    highest = lax.Precision.HIGHEST
    levels, cols_y, cols_x = forcing_field.shape
    groups_x = lax.axis_size("gx")
    groups_y = lax.axis_size("gy")
    devices_all = groups_x * groups_y
    full_x = cols_x * groups_x
    full_y = cols_y * groups_y
    row_total = innovations.shape[0]
    capacity = 2 * row_total // devices_all
    targets = owner_device[:, 0]
    one_hot = (targets[:, None] == jnp.arange(devices_all, dtype=jnp.int32)[None, :]).astype(
        jnp.int32
    )
    rank_in_peer = jnp.sum(jnp.cumsum(one_hot, axis=0) * one_hot, axis=1) - 1
    slot_index = targets * capacity + rank_in_peer
    payload = jnp.dot(
        innovations, obs_weight, precision=highest, preferred_element_type=jnp.float32
    )
    send_rows = jnp.zeros((devices_all * capacity, levels), jnp.float32).at[slot_index].set(payload)
    send_cols = jnp.full((devices_all * capacity,), -1, jnp.int32).at[slot_index].set(column_index)
    send_rows = send_rows.reshape(groups_x, groups_y, capacity, levels)
    send_cols = send_cols.reshape(groups_x, groups_y, capacity)
    got_rows, got_cols = (
        lax.all_to_all(
            lax.all_to_all(send_rows, "gx", split_axis=0, concat_axis=0, tiled=True),
            "gy",
            split_axis=1,
            concat_axis=1,
            tiled=True,
        ),
        lax.all_to_all(
            lax.all_to_all(send_cols, "gx", split_axis=0, concat_axis=0, tiled=True),
            "gy",
            split_axis=1,
            concat_axis=1,
            tiled=True,
        ),
    )
    flat_rows = got_rows.reshape(devices_all * capacity, levels)
    flat_cols = got_cols.reshape(devices_all * capacity)
    row_valid = flat_cols >= 0
    summed = jax.ops.segment_sum(
        jnp.where(row_valid[:, None], flat_rows, 0.0),
        jnp.where(row_valid, flat_cols, 0),
        num_segments=cols_y * cols_x,
    )
    observed = summed.reshape(cols_y, cols_x, levels).transpose(2, 0, 1)
    forcing_total = forcing_field + observed
    vertical = jnp.einsum("mz,zyx->myx", vert_inverse, forcing_total, precision=highest)
    table_x = cosine_table(full_x)
    table_y = cosine_table(full_y)
    line_y = eigen_line(jnp.arange(full_y, dtype=jnp.float32), full_y)
    along_x = lax.all_to_all(vertical, "gx", split_axis=0, concat_axis=2, tiled=True)
    along_x = jnp.einsum("myx,kx->mky", along_x, table_x, precision=highest)
    along_y = lax.all_to_all(along_x, "gy", split_axis=1, concat_axis=2, tiled=True)
    along_y = jnp.einsum("mky,ly->mkl", along_y, table_y, precision=highest)
    level_count = levels // groups_x
    wave_count = full_x // groups_y
    level_eigen = lax.dynamic_slice_in_dim(
        vert_eigen, lax.axis_index("gx") * level_count, level_count
    )
    wave_ids = (lax.axis_index("gy") * wave_count + jnp.arange(wave_count, dtype=jnp.int32)).astype(
        jnp.float32
    )
    line_x = eigen_line(wave_ids, full_x)
    denominator = level_eigen[:, None, None] + line_x[None, :, None] + line_y[None, None, :]
    solved = along_y / denominator
    back_lines = jnp.einsum("mkl,ly->mky", solved, table_y, precision=highest)
    back_lines = lax.all_to_all(back_lines, "gy", split_axis=2, concat_axis=1, tiled=True)
    back_lines = jnp.einsum("mky,kx->myx", back_lines, table_x, precision=highest)
    physical = lax.all_to_all(back_lines, "gx", split_axis=2, concat_axis=0, tiled=True)
    return jnp.einsum("zm,myx->zyx", vert_basis, physical, precision=highest)


def solution(mesh):
    return jax.shard_map(
        per_device,
        mesh=mesh,
        in_specs=(
            P(None, "gy", "gx"),
            P(("gx", "gy"), None),
            P(("gx", "gy"), None),
            P(("gx", "gy")),
            P(),
            P(),
            P(),
            P(),
        ),
        out_specs=P(None, "gy", "gx"),
        check_vma=False,
    )
```

profile of v0, /device:TPU:1, one launch (start us, length us, event | category | flops | bytes accessed | tf_op | source)
XLA Modules:
  0.0 398.9 jit_solution(1919015030830153475)
XLA Ops:
  3.7 8.2 %scatter_custom_fusion = s32[4096]{0:T(1024)S(1)} fusion(s32[2048]{0:T(1024)S(1)} %bitcast.110, s32[2048]{0:T(1024)} %param.11, s32[]{:T(128)} %constant.26.clone.1), kind=kCustom, calls=%fused_computation.60 | custom fusion | bytes 16896 | tf_op jit(solution)/shard_map/scatter | solution.py:47
  12.8 6.5 %all-to-all-start = ((s32[8,1,512]{2,1,0:T(1,128)}), s32[8,1,512]{2,1,0:T(1,128)S(1)}, u32[]{:S(2)}, u32[]{:S(2)}) async-start(s32[8,1,512]{2,1,0:T(1,128)} %reshape.171), calls=%async_computation | async-start | bytes 32768 | tf_op jit(solution)/shard_map/all_to_all | solution.py:59
  22.1 6.5 %scatter_custom_fusion.1 = f32[4096,64]{1,0:T(8,128)S(1)} fusion(s32[2048]{0:T(1024)S(1)} %bitcast.111, f32[2048,64]{1,0:T(8,128)} %fusion.50, f32[]{:T(128)} %constant.19.clone.1), kind=kCustom, calls=%fused_computation.50 | custom fusion | bytes 1049088 | tf_op jit(solution)/shard_map/scatter | solution.py:46
  30.7 4.8 %all-to-all-start.2 = ((f32[8,1,32768]{2,1,0:T(1,128)}), f32[8,1,32768]{2,1,0:T(1,128)S(1)}, u32[]{:S(2)}, u32[]{:S(2)}) async-start(f32[8,1,32768]{2,1,0:T(1,128)} %reshape.175), calls=%async_computation.2 | async-start | bytes 2097152 | tf_op jit(solution)/shard_map/all_to_all | solution.py:52
  37.6 13.0 %all-to-all-done.2 = f32[8,1,32768]{2,1,0:T(1,128)S(1)} async-done(((f32[8,1,32768]{2,1,0:T(1,128)}), f32[8,1,32768]{2,1,0:T(1,128)S(1)}, u32[]{:S(2)}, u32[]{:S(2)}) %all-to-all-start.2) | async-done | bytes 1048608 | tf_op jit(solution)/shard_map/all_to_all | solution.py:52
  50.6 10.7 %all-to-all-start.1 = ((s32[32,1,128]{2,1,0:T(1,128)}), s32[32,1,128]{2,1,0:T(1,128)S(1)}, u32[]{:S(2)}, u32[]{:S(2)}) async-start(s32[32,1,128]{2,1,0:T(1,128)} %reshape.173), calls=%async_computation.1 | async-start | bytes 32768 | tf_op jit(solution)/shard_map/all_to_all | solution.py:58
  61.8 4.4 %reduce.2 = f32[8,32768]{1,0:T(8,128)} reduce(f32[8,1,32768]{2,1,0:T(1,128)S(1)} %all-to-all-done.2, f32[]{:T(128)} %broadcast.197), dimensions={1}, to_apply=%all_to_all.66.reduce_sub_computation | reduce | bytes 2097156 | tf_op jit(solution)/shard_map/all_to_all | solution.py:52
  73.4 9.7 %all-to-all-start.3 = ((f32[32,1,8192]{2,1,0:T(1,128)}), f32[32,1,8192]{2,1,0:T(1,128)S(1)}, u32[]{:S(2)}, u32[]{:S(2)}) async-start(f32[32,1,8192]{2,1,0:T(1,128)} %reshape.177), calls=%async_computation.3 | async-start | bytes 2097152 | tf_op jit(solution)/shard_map/all_to_all | solution.py:51
  84.4 23.2 %all-to-all-done.3 = f32[32,1,8192]{2,1,0:T(1,128)S(1)} async-done(((f32[32,1,8192]{2,1,0:T(1,128)}), f32[32,1,8192]{2,1,0:T(1,128)S(1)}, u32[]{:S(2)}, u32[]{:S(2)}) %all-to-all-start.3) | async-done | bytes 1048608 | tf_op jit(solution)/shard_map/all_to_all | solution.py:51
  107.7 4.3 %reduce.3 = f32[32,8192]{1,0:T(8,128)} reduce(f32[32,1,8192]{2,1,0:T(1,128)S(1)} %all-to-all-done.3, f32[]{:T(128)} %broadcast.197), dimensions={1}, to_apply=%all_to_all.67.reduce_sub_computation | reduce | bytes 2097156 | tf_op jit(solution)/shard_map/all_to_all | solution.py:51
  117.4 23.3 %scatter_custom_fusion.2 = f32[4096,64]{1,0:T(8,128)S(1)} fusion(s32[4096]{0:T(1024)S(1)} %bitcast.109, f32[4096,64]{1,0:T(8,128)} %bitcast_select_fusion.1, f32[]{:T(128)} %constant.19.clone.1), kind=kCustom, calls=%fused_computation.48 | custom fusion | flops 262144 | bytes 1049088 | tf_op jit(solution)/shard_map/scatter-add | solution.py:69
  147.5 8.9 %all-to-all-start.4 = ((f32[64,32,128]{2,1,0:T(8,128)}), f32[64,32,128]{2,1,0:T(8,128)S(1)}, u32[]{:S(2)}, u32[]{:S(2)}) async-start(f32[64,32,128]{2,1,0:T(8,128)} %copy.57), calls=%async_computation.4 | async-start | bytes 2097152 | tf_op jit(solution)/shard_map/all_to_all | solution.py:80
  156.5 14.9 %all-to-all-done.4 = f32[64,32,128]{2,1,0:T(8,128)S(1)} async-done(((f32[64,32,128]{2,1,0:T(8,128)}), f32[64,32,128]{2,1,0:T(8,128)S(1)}, u32[]{:S(2)}, u32[]{:S(2)}) %all-to-all-start.4) | async-done | bytes 1048608 | tf_op jit(solution)/shard_map/all_to_all | solution.py:80
  173.1 19.5 %fusion.27 = f32[8,1024,32]{1,2,0:T(8,128)S(1)} fusion(f32[8,32,1024]{2,1,0:T(8,128)} %all_to_all.71, f32[1024]{0:T(1024)S(1)} %get-tuple-element.5, f32[1024]{0:T(1024)S(1)} %get-tuple-element.6, f32[1024]{0:T(1024)S(1)} %get-tuple-element.8), kind=kOutput, calls=%fused_computation.37 | convolution fusion | flops 3224371200 | bytes 2109440 | tf_op jit(solution)/shard_map/myx,kx->mky/dot_general | solution.py:81
  195.3 4.7 %reshape.179 = f32[32,1,8192]{2,1,0:T(1,128)} reshape(f32[1024,8,32]{2,1,0:T(8,128)} %bitcast.87) | data formatting | bytes 2097152
  200.0 5.2 %all-to-all-start.5 = ((f32[32,1,8192]{2,1,0:T(1,128)}), f32[32,1,8192]{2,1,0:T(1,128)S(1)}, u32[]{:S(2)}, u32[]{:S(2)}) async-start(f32[32,1,8192]{2,1,0:T(1,128)} %reshape.179), calls=%async_computation.5 | async-start | bytes 2097152 | tf_op jit(solution)/shard_map/all_to_all | solution.py:82
  205.5 24.5 %all-to-all-done.5 = f32[32,1,8192]{2,1,0:T(1,128)S(1)} async-done(((f32[32,1,8192]{2,1,0:T(1,128)}), f32[32,1,8192]{2,1,0:T(1,128)S(1)}, u32[]{:S(2)}, u32[]{:S(2)}) %all-to-all-start.5) | async-done | bytes 1048608 | tf_op jit(solution)/shard_map/all_to_all | solution.py:82
  235.8 6.6 %copy.74 = f32[8,32,32,32]{3,1,2,0:T(8,128)} copy(f32[8,32,32,32]{3,0,2,1:T(8,128)} %bitcast.91) | data formatting | bytes 2097152 | tf_op jit(solution)/shard_map/all_to_all | solution.py:82
  246.3 17.9 %fusion.4 = f32[8,32,1024]{2,1,0:T(8,128)S(1)} fusion(f32[8,32,1024]{2,1,0:T(8,128)S(1)} %all_to_all.75, f32[1024]{0:T(1024)S(1)} %get-tuple-element.5, f32[1024]{0:T(1024)S(1)} %get-tuple-element.6, f32[1024]{0:T(1024)S(1)} %get-tuple-element.8), kind=kOutput, calls=%fused_computation.7 | convolution fusion | flops 3224371200 | bytes 2109440 | tf_op jit(solution)/shard_map/mky,ly->mkl/dot_general | solution.py:83
  264.2 18.5 %fusion.2 = f32[8,32,1024]{2,1,0:T(8,128)S(1)} fusion(f32[1024]{0:T(1024)S(1)} %get-tuple-element.5, f32[1024]{0:T(1024)S(1)} %get-tuple-element.6, f32[1024]{0:T(1024)S(1)} %get-tuple-element.8, f32[8,32,1024]{2,1,0:T(8,128)S(1)} %fusion.4, f32[1024]{0:T(1024)S(1)} %get-tuple-element.7, f32[8,32]{1,0:T(8,128)S(1)} %broadcast_add_fusion.2), kind=kOutput, calls=%fused_computation.5 | convolution fusion | flops 3224895488 | bytes 2114560 | tf_op jit(solution)/shard_map/mkl,ly->mky/dot_general | solution.py:95
  289.2 33.1 %all_to_all.92 = f32[32,1,8192]{2,1,0:T(1,128)S(1)} all-to-all(f32[32,1,8192]{2,1,0:T(1,128)S(1)} %reshape.181), channel_id=1, replica_groups=mesh['gx'=8,'gy'=32] {'gy'}, dimensions={0} | all-to-all | bytes 2097152 | tf_op jit(solution)/shard_map/all_to_all | solution.py:96
  328.2 6.6 %copy.73 = f32[8,32,32,32]{1,2,3,0:T(8,128)} copy(f32[8,32,32,32]{1,0,3,2:T(8,128)} %bitcast.93) | data formatting | bytes 2097152 | tf_op jit(solution)/shard_map/all_to_all | solution.py:96
  338.7 18.0 %fusion = f32[8,32,1024]{2,1,0:T(8,128)S(1)} fusion(f32[8,1024,32]{1,2,0:T(8,128)S(1)} %all_to_all.79, f32[1024]{0:T(1024)S(1)} %get-tuple-element.5, f32[1024]{0:T(1024)S(1)} %get-tuple-element.6, f32[1024]{0:T(1024)S(1)} %get-tuple-element.8), kind=kOutput, calls=%fused_computation.3 | convolution fusion | flops 3224371200 | bytes 2109440 | tf_op jit(solution)/shard_map/mky,kx->myx/dot_general | solution.py:97
  363.3 22.8 %all_to_all.93 = f32[8,1,32768]{2,1,0:T(1,128)S(1)} all-to-all(f32[8,1,32768]{2,1,0:T(1,128)S(1)} %reshape.183), channel_id=1, replica_groups=mesh['gx'=8,'gy'=32] {'gx'}, dimensions={0} | all-to-all | bytes 2097152 | tf_op jit(solution)/shard_map/all_to_all | solution.py:98
  (79 shorter events, 82.1 us)
Async XLA Ops:
  0.0 19.3 %copy-start = (f32[2048,64]{0,1:T(8,128)S(1)}, f32[2048,64]{0,1:T(8,128)}, u32[]{:S(2)}) copy-start(f32[2048,64]{0,1:T(8,128)} %param.9) | copy-start | bytes 1572868
  1.3 1.5 copy-start.2
  1.5 17.8 %copy-start.5 = (f32[64,64]{1,0:T(8,128)S(1)}, f32[64,64]{1,0:T(8,128)}, u32[]{:S(2)}) copy-start(f32[64,64]{1,0:T(8,128)} %param.12) | copy-start | bytes 49156
  12.8 17.9 %all-to-all-start = ((s32[8,1,512]{2,1,0:T(1,128)}), s32[8,1,512]{2,1,0:T(1,128)S(1)}, u32[]{:S(2)}, u32[]{:S(2)}) async-start(s32[8,1,512]{2,1,0:T(1,128)} %reshape.171), calls=%async_computation | async-start | bytes 32768 | tf_op jit(solution)/shard_map/all_to_all | solution.py:59
  30.7 19.9 %all-to-all-start.2 = ((f32[8,1,32768]{2,1,0:T(1,128)}), f32[8,1,32768]{2,1,0:T(1,128)S(1)}, u32[]{:S(2)}, u32[]{:S(2)}) async-start(f32[8,1,32768]{2,1,0:T(1,128)} %reshape.175), calls=%async_computation.2 | async-start | bytes 2097152 | tf_op jit(solution)/shard_map/all_to_all | solution.py:52
  50.6 22.8 %all-to-all-start.1 = ((s32[32,1,128]{2,1,0:T(1,128)}), s32[32,1,128]{2,1,0:T(1,128)S(1)}, u32[]{:S(2)}, u32[]{:S(2)}) async-start(s32[32,1,128]{2,1,0:T(1,128)} %reshape.173), calls=%async_computation.1 | async-start | bytes 32768 | tf_op jit(solution)/shard_map/all_to_all | solution.py:58
  73.4 34.3 %all-to-all-start.3 = ((f32[32,1,8192]{2,1,0:T(1,128)}), f32[32,1,8192]{2,1,0:T(1,128)S(1)}, u32[]{:S(2)}, u32[]{:S(2)}) async-start(f32[32,1,8192]{2,1,0:T(1,128)} %reshape.177), calls=%async_computation.3 | async-start | bytes 2097152 | tf_op jit(solution)/shard_map/all_to_all | solution.py:51
  117.4 26.8 %copy-start.3 = (f32[64,64]{1,0:T(8,128)S(1)}, f32[64,64]{1,0:T(8,128)}, u32[]{:S(2)}) copy-start(f32[64,64]{1,0:T(8,128)} %param.13) | copy-start | bytes 49156
  147.5 23.9 %all-to-all-start.4 = ((f32[64,32,128]{2,1,0:T(8,128)}), f32[64,32,128]{2,1,0:T(8,128)S(1)}, u32[]{:S(2)}, u32[]{:S(2)}) async-start(f32[64,32,128]{2,1,0:T(8,128)} %copy.57), calls=%async_computation.4 | async-start | bytes 2097152 | tf_op jit(solution)/shard_map/all_to_all | solution.py:80
  195.3 10.0 %copy-start.6 = (f32[64]{0:T(128)S(1)}, f32[64]{0:T(128)}, u32[]{:S(2)}) copy-start(f32[64]{0:T(128)} %param.15) | copy-start | bytes 772
  200.0 29.9 %all-to-all-start.5 = ((f32[32,1,8192]{2,1,0:T(1,128)}), f32[32,1,8192]{2,1,0:T(1,128)S(1)}, u32[]{:S(2)}, u32[]{:S(2)}) async-start(f32[32,1,8192]{2,1,0:T(1,128)} %reshape.179), calls=%async_computation.5 | async-start | bytes 2097152 | tf_op jit(solution)/shard_map/all_to_all | solution.py:82
  389.1 6.6 %copy-start.4 = (f32[64,64]{1,0:T(8,128)S(1)}, f32[64,64]{1,0:T(8,128)}, u32[]{:S(2)}) copy-start(f32[64,64]{1,0:T(8,128)} %param.14) | copy-start | bytes 49156
  392.4 5.9 %copy-start.1 = (f32[2048,64]{0,1:T(8,128)S(1)}, f32[2048,64]{0,1:T(8,128)}, u32[]{:S(2)}) copy-start(f32[2048,64]{0,1:T(8,128)} %param.9) | copy-start | bytes 1572868
where the time goes:
time: 406 us; the launch traced here: 399 us
  local copies, waits for them, and re-layouts  91.9 us (23%)
  matrix products  79.4 us (20%)
  waiting for transfers between devices  75.6 us (19%)
  blocking collectives  55.9 us (14%)
  other arithmetic  49.3 us (12%)
  starting transfers between devices  45.9 us (11%)
    all_to_all x1, blocking collectives, per_device(): lax.all_to_all(back_lines, 'gy', split_axis=2, concat_axis=1, tiled=True)  33.1 us
    unnamed x28, local copies, waits for them, and re-layouts  32.5 us
    all_to_all x1, waiting for transfers between devices, per_device(): lax.all_to_all(along_x, 'gy', split_axis=1, concat_axis=2, tiled=True)  24.5 us
    scatter-add x1, other arithmetic, per_device(): jax.ops.segment_sum(jnp.where(row_valid[:, None], flat_rows, 0.0), jnp.wh...  23.3 us
    all_to_all x1, waiting for transfers between devices, per_device(): lax.all_to_all(lax.all_to_all(send_rows, 'gx', split_axis=0, concat_axis=...  23.2 us
    all_to_all x1, blocking collectives, per_device(): lax.all_to_all(back_lines, 'gx', split_axis=2, concat_axis=0, tiled=True)  22.8 us
    dot_general x1, matrix products, per_device(): along_x = jnp.einsum('myx,kx->mky', along_x, table_x, precision=highest)  19.5 us
    dot_general x1, matrix products, per_device(): back_lines = jnp.einsum('mkl,ly->mky', solved, table_y, precision=highest)  18.5 us
  transfers between devices with their start and end apart: 6, of which 4 were waited for; matrix products, arithmetic and copies ran while one was open for 7% of the time, Pallas kernels for 0%

commit v1 on v0

v1 whole, which is shorter than its diff:
```python
import functools

import jax
import jax.numpy as jnp
import ml_dtypes
import numpy as np
from jax import lax
from jax.experimental import pallas as pl
from jax.experimental.pallas import tpu as pltpu
from jax.sharding import PartitionSpec as P

MESH = pl.DeviceIdType.MESH
F32 = jnp.float32
BF16 = jnp.bfloat16
LANES = 128
Y_CUTS = 2
K_CUTS = 2


def wave_order(length):
    return np.concatenate([np.arange(0, length, 2), np.arange(1, length, 2)])


def split_table(table):
    high = table.astype(np.float32).astype(ml_dtypes.bfloat16)
    low = (table - high.astype(np.float64)).astype(np.float32).astype(ml_dtypes.bfloat16)
    return high, low


def wave_tables(length):
    waves = wave_order(length).astype(np.float64)
    points = np.arange(length, dtype=np.float64)
    scales = np.where(waves == 0, np.sqrt(1.0 / length), np.sqrt(2.0 / length))
    table = scales[:, None] * np.cos(np.pi * waves[:, None] * (2 * points + 1) / (2 * length))
    line = 4.0 * np.sin(np.pi * waves / (2.0 * length)) ** 2
    return split_table(table), split_table(table.T), line.astype(np.float32)


def halves(value):
    high = value.astype(BF16)
    low = (value - high.astype(F32)).astype(BF16)
    return high, low


def dot(left, right):
    return jnp.dot(left, right, preferred_element_type=F32)


def wait_for(ref, sem):
    pltpu.make_async_copy(ref, ref, sem).wait()


def field_kernel(
    n_gx, n_gy, gy_dims, field, vinv, vbas, eigen, c_hi, c_lo, t_hi, t_lo, line_col, line_row, out,
    vert, x_in, x_out, y_in, y_out, z_in, z_out, phys, solved,
    xf_send, xf_recv, yf_send, yf_recv, yb_send, yb_recv, xb_send, xb_recv,
):
    gx = lax.axis_index("gx")
    gy = lax.axis_index("gy")
    n_hi, n_lo = gy_dims
    rows_y = y_in.shape[2]
    levels = phys.shape[0] // rows_y
    own_levels = levels // n_gx
    parts = n_gy // own_levels
    cut = rows_y // Y_CUTS
    length = c_hi.shape[0]

    def gx_peer(step):
        return lax.rem(gx + step, n_gx)

    def gy_peer(step):
        high = lax.rem(gy // n_lo + step // n_lo, n_hi)
        low = lax.rem(gy + step, n_lo)
        return high * n_lo + low

    barrier = pltpu.get_barrier_semaphore()

    def greet_gx(step, carry):
        pl.semaphore_signal(barrier, inc=1, device_id=(gx_peer(step), gy), device_id_type=MESH)
        return carry

    def greet_gy(step, carry):
        pl.semaphore_signal(barrier, inc=1, device_id=(gx, gy_peer(step)), device_id_type=MESH)
        return carry

    lax.fori_loop(1, n_gx, greet_gx, 0)
    lax.fori_loop(1, n_gy, greet_gy, 0)

    def mix_levels(matrix, source, target, y_cut):
        m_hi, m_lo = halves(matrix)
        stack = jnp.concatenate([m_hi, m_hi, m_lo], axis=1)
        for y in range(y_cut * cut, (y_cut + 1) * cut, 2):
            pair = jnp.concatenate(
                [source[pl.ds(y + i, levels, stride=rows_y), :] for i in range(2)], axis=1
            )
            hi, lo = halves(pair)
            mixed = dot(stack, jnp.concatenate([hi, lo, hi], axis=0))
            for i in range(2):
                target[pl.ds(y + i, levels, stride=rows_y), :] = mixed[:, i * LANES : (i + 1) * LANES]

    def send_gx(source, target, send_sem, recv_sem):
        pltpu.make_async_copy(source(gx), target, recv_sem).start()

        def one(step, carry):
            peer = gx_peer(step)
            pltpu.make_async_remote_copy(
                src_ref=source(peer), dst_ref=target, send_sem=send_sem, recv_sem=recv_sem,
                device_id=(peer, gy), device_id_type=MESH,
            ).start()
            return carry

        lax.fori_loop(1, n_gx, one, 0)

    def send_gy(source, target, send_sem, recv_sem):
        pltpu.make_async_copy(source(gy), target, recv_sem).start()

        def one(step, carry):
            peer = gy_peer(step)
            pltpu.make_async_remote_copy(
                src_ref=source(peer), dst_ref=target, send_sem=send_sem, recv_sem=recv_sem,
                device_id=(gx, peer), device_id_type=MESH,
            ).start()
            return carry

        lax.fori_loop(1, n_gy, one, 0)

    def y_span(y_cut):
        return pl.ds(y_cut * cut, cut)

    vert3 = vert.reshape(levels, rows_y, LANES)
    phys3 = phys.reshape(levels, rows_y, LANES)

    for h in range(Y_CUTS):
        mix_levels(vinv[...], field, vert, h)
        if h == 0:
            pl.semaphore_wait(barrier, n_gx - 1 + n_gy - 1)
        send_gx(
            lambda a: vert3.at[pl.ds(a * own_levels, own_levels), y_span(h), :],
            x_in.at[gx, :, y_span(h), :],
            xf_send.at[h], xf_recv.at[h],
        )

    wide = 2 * LANES

    def transform_x(h, k):
        lines = jnp.concatenate(
            [x_in[a, :, y_span(h), :].reshape(own_levels * cut, LANES) for a in range(n_gx)], axis=1
        )
        hi, lo = halves(lines)
        for block in range(parts * LANES // wide):
            cols = pl.ds(k * parts * LANES + block * wide, wide)
            res = dot(hi, t_hi[:, cols]) + dot(lo, t_hi[:, cols]) + dot(hi, t_lo[:, cols])
            for i in range(2):
                x_out[k, :, block * 2 + i, y_span(h), :] = res[:, i * LANES : (i + 1) * LANES].reshape(
                    own_levels, cut, LANES
                )
        send_gy(
            lambda b: x_out.at[k, b // parts, lax.rem(b, parts), y_span(h), :],
            y_in.at[k, gy, y_span(h), :],
            yf_send.at[k, h], yf_recv.at[k, h],
        )

    for k in range(K_CUTS):
        for h in range(Y_CUTS):
            if k == 0:
                wait_for(x_in.at[:, :, y_span(h), :], xf_recv.at[h])
            transform_x(h, k)

    level = gx * own_levels + gy // parts
    part = lax.rem(gy, parts)

    def transform_y(k):
        hi, lo = halves(y_in[k].reshape(length, LANES))
        both = jnp.concatenate([hi, lo], axis=1)
        line = line_row[pl.ds(k * parts + part, 1), :] + eigen[level]
        for block in range(length // wide):
            rows = pl.ds(block * wide, wide)
            res = dot(c_hi[rows, :], both)
            res = res[:, :LANES] + res[:, LANES:] + dot(c_lo[rows, :], hi)
            res = res / (line_col[rows, :] + line)
            s_hi, s_lo = halves(res)
            solved[rows, :LANES] = s_hi
            solved[rows, LANES:] = s_lo
        per = wide // rows_y
        for block in range(length // wide):
            rows = pl.ds(block * wide, wide)
            res = dot(t_hi[rows, :], solved[...])
            res = res[:, :LANES] + res[:, LANES:] + dot(t_lo[rows, :], solved[:, :LANES])
            y_out[k, pl.ds(block * per, per), :, :] = res.reshape(per, rows_y, LANES)

    for k in range(K_CUTS):
        for h in range(Y_CUTS):
            wait_for(y_in.at[k, :, y_span(h), :], yf_recv.at[k, h])
        transform_y(k)
        for h in range(Y_CUTS):
            send_gy(
                lambda b: y_out.at[k, b, y_span(h), :],
                z_in.at[k, gy // parts, part, y_span(h), :],
                yb_send.at[k, h], yb_recv.at[k, h],
            )

    for h in range(Y_CUTS):
        for k in range(K_CUTS):
            wait_for(z_in.at[k, :, :, y_span(h), :], yb_recv.at[k, h])
        lines = jnp.concatenate(
            [
                z_in[k, :, p, y_span(h), :].reshape(own_levels * cut, LANES)
                for k in range(K_CUTS)
                for p in range(parts)
            ],
            axis=1,
        )
        hi, lo = halves(lines)
        for block in range(length // wide):
            cols = pl.ds(block * wide, wide)
            res = dot(hi, c_hi[:, cols]) + dot(lo, c_hi[:, cols]) + dot(hi, c_lo[:, cols])
            for i in range(2):
                z_out[block * 2 + i, :, y_span(h), :] = res[:, i * LANES : (i + 1) * LANES].reshape(
                    own_levels, cut, LANES
                )
        send_gx(
            lambda a: z_out.at[a, :, y_span(h), :],
            phys3.at[pl.ds(gx * own_levels, own_levels), y_span(h), :],
            xb_send.at[h], xb_recv.at[h],
        )

    for h in range(Y_CUTS):
        wait_for(phys3.at[:, y_span(h), :], xb_recv.at[h])
        mix_levels(vbas[...], phys, out, h)

    for h in range(Y_CUTS):
        wait_for(x_in.at[pl.ds(0, n_gx - 1), :, y_span(h), :], xf_send.at[h])
        wait_for(z_out.at[pl.ds(0, n_gx - 1), :, y_span(h), :], xb_send.at[h])
        for k in range(K_CUTS):
            wait_for(y_in.at[k, pl.ds(0, n_gy - 1), y_span(h), :], yf_send.at[k, h])
            wait_for(y_out.at[k, pl.ds(0, n_gy - 1), y_span(h), :], yb_send.at[k, h])


def solve_field(forcing_total, vert_inverse, vert_basis, vert_eigen, gy_dims):
    n_gx = lax.axis_size("gx")
    n_gy = lax.axis_size("gy")
    levels, rows_y, cols_x = forcing_total.shape
    length = cols_x * n_gx
    (c_hi, c_lo), (t_hi, t_lo), line = wave_tables(length)
    own_levels = levels // n_gx
    parts = n_gy // own_levels
    line_col = np.broadcast_to(line[:, None], (length, LANES))
    line_row = line.reshape(K_CUTS * parts, LANES)
    vmem = pl.BlockSpec(memory_space=pltpu.VMEM)
    smem = pl.BlockSpec(memory_space=pltpu.SMEM)
    dma = pltpu.SemaphoreType.DMA
    out = pl.pallas_call(
        functools.partial(field_kernel, n_gx, n_gy, gy_dims),
        out_shape=jax.ShapeDtypeStruct((levels * rows_y, cols_x), F32),
        in_specs=[vmem, vmem, vmem, smem, vmem, vmem, vmem, vmem, vmem, vmem],
        out_specs=vmem,
        scratch_shapes=[
            pltpu.VMEM((levels * rows_y, LANES), F32),
            pltpu.VMEM((n_gx, own_levels, rows_y, LANES), F32),
            pltpu.VMEM((K_CUTS, own_levels, parts, rows_y, LANES), F32),
            pltpu.VMEM((K_CUTS, n_gy, rows_y, LANES), F32),
            pltpu.VMEM((K_CUTS, n_gy, rows_y, LANES), F32),
            pltpu.VMEM((K_CUTS, own_levels, parts, rows_y, LANES), F32),
            pltpu.VMEM((n_gx, own_levels, rows_y, LANES), F32),
            pltpu.VMEM((levels * rows_y, LANES), F32),
            pltpu.VMEM((length, 2 * LANES), BF16),
            dma((Y_CUTS,)), dma((Y_CUTS,)),
            dma((K_CUTS, Y_CUTS)), dma((K_CUTS, Y_CUTS)),
            dma((K_CUTS, Y_CUTS)), dma((K_CUTS, Y_CUTS)),
            dma((Y_CUTS,)), dma((Y_CUTS,)),
        ],
        compiler_params=pltpu.CompilerParams(
            collective_id=0, has_side_effects=True, vmem_limit_bytes=48 * 1024 * 1024
        ),
        name="field_solve",
    )(
        forcing_total.reshape(levels * rows_y, cols_x), vert_inverse, vert_basis, vert_eigen,
        c_hi, c_lo, t_hi, t_lo, line_col, line_row,
    )
    return out.reshape(levels, rows_y, cols_x)


def observed_field(innovations, owner_device, column_index, obs_weight, shape):
    highest = lax.Precision.HIGHEST
    levels, cols_y, cols_x = shape
    groups_x = lax.axis_size("gx")
    groups_y = lax.axis_size("gy")
    devices_all = groups_x * groups_y
    row_total = innovations.shape[0]
    capacity = 2 * row_total // devices_all
    targets = owner_device[:, 0]
    one_hot = (targets[:, None] == jnp.arange(devices_all, dtype=jnp.int32)[None, :]).astype(
        jnp.int32
    )
    rank_in_peer = jnp.sum(jnp.cumsum(one_hot, axis=0) * one_hot, axis=1) - 1
    slot_index = targets * capacity + rank_in_peer
    payload = jnp.dot(innovations, obs_weight, precision=highest, preferred_element_type=F32)
    send_rows = jnp.zeros((devices_all * capacity, levels), F32).at[slot_index].set(payload)
    send_cols = jnp.full((devices_all * capacity,), -1, jnp.int32).at[slot_index].set(column_index)
    send_rows = send_rows.reshape(groups_x, groups_y, capacity, levels)
    send_cols = send_cols.reshape(groups_x, groups_y, capacity)

    def swap(array):
        array = lax.all_to_all(array, "gx", split_axis=0, concat_axis=0, tiled=True)
        return lax.all_to_all(array, "gy", split_axis=1, concat_axis=1, tiled=True)

    flat_rows = swap(send_rows).reshape(devices_all * capacity, levels)
    flat_cols = swap(send_cols).reshape(devices_all * capacity)
    row_valid = flat_cols >= 0
    summed = jax.ops.segment_sum(
        jnp.where(row_valid[:, None], flat_rows, 0.0),
        jnp.where(row_valid, flat_cols, 0),
        num_segments=cols_y * cols_x,
    )
    return summed.reshape(cols_y, cols_x, levels).transpose(2, 0, 1)


def per_device(
    forcing_field, innovations, owner_device, column_index, obs_weight, vert_inverse, vert_basis,
    vert_eigen,
):
    observed = observed_field(
        innovations, owner_device, column_index, obs_weight, forcing_field.shape
    )
    return solve_field(forcing_field + observed, vert_inverse, vert_basis, vert_eigen, (4, 8))


def solution(mesh):
    return jax.shard_map(
        per_device,
        mesh=mesh,
        in_specs=(
            P(None, "gy", "gx"),
            P(("gx", "gy"), None),
            P(("gx", "gy"), None),
            P(("gx", "gy")),
            P(),
            P(),
            P(),
            P(),
        ),
        out_specs=P(None, "gy", "gx"),
        check_vma=False,
    )
```

time: 406 us -> 226 us (0.56); the launches traced: 399 us -> 225 us
  Pallas kernels: 0 us -> 80 us
  matrix products: 79.4 us -> 2.78 us
  local copies, waits for them, and re-layouts: 91.9 us -> 34.7 us
  blocking collectives: 55.9 us -> 0 us
  waiting for transfers between devices: 75.6 us -> 36.2 us
  starting transfers between devices: 45.9 us -> 31 us
  other arithmetic: 49.3 us -> 40.4 us
    pallas_call x0 -> x1, Pallas kernels: none -> 80 us  [solve_field(): pl.pallas_call(functools.partial(field_kernel, n_gx, n_gy, gy_dims), out_...]
    dot_general x7 -> x1, matrix products: 79.4 us -> 2.78 us  [observed_field(): jnp.dot(innovations, obs_weight, precision=highest, preferred_element_typ...]
    all_to_all x2 -> x0, blocking collectives: 55.9 us -> none  [the longest x1 33.1 us: per_device(): lax.all_to_all(back_lines, 'gy', split_axis=2, concat_axis=1, tiled=True)]
    all_to_all x6 -> x4, waiting for transfers between devices: 75.6 us -> 36.2 us  [the longest x2 23.2 us: swap(): return lax.all_to_all(array, 'gy', split_axis=1, concat_axis=1, tiled=True)]
    all_to_all x14 -> x7, local copies, waits for them, and re-layouts: 29.1 us -> 3.11 us  [the longest x4 2.81 us: swap(): array = lax.all_to_all(array, 'gx', split_axis=0, concat_axis=0, tiled=True)]
    unnamed x28 -> x27, local copies, waits for them, and re-layouts: 32.5 us -> 12.3 us
    all_to_all x6 -> x4, starting transfers between devices: 45.9 us -> 31 us  [the longest x2 19.7 us: swap(): return lax.all_to_all(array, 'gy', split_axis=1, concat_axis=1, tiled=True)]
    all_to_all x7 -> x4, other arithmetic: 19.4 us -> 10.1 us  [the longest x2 5.12 us: swap(): array = lax.all_to_all(array, 'gx', split_axis=0, concat_axis=0, tiled=True)]
  transfers between devices with their start and end apart: 6 -> 4, of which waited for: 4 -> 2; matrix products, arithmetic and copies ran while one was open for 7% -> 12% of each run, Pallas kernels for 0% -> 0%
where the time goes in v1:
time: 226 us; the launch traced here: 225 us
  Pallas kernels  80 us (35%)
  other arithmetic  40.4 us (18%)
  waiting for transfers between devices  36.2 us (16%)
  local copies, waits for them, and re-layouts  34.7 us (15%)
  starting transfers between devices  31 us (14%)
  matrix products  2.78 us (1%)
    pallas_call x1, Pallas kernels, solve_field(): pl.pallas_call(functools.partial(field_kernel, n_gx, n_gy, gy_dims), out_...  80 us
    scatter-add x1, other arithmetic, observed_field(): jax.ops.segment_sum(jnp.where(row_valid[:, None], flat_rows, 0.0), jnp.wh...  23.7 us
    all_to_all x2, waiting for transfers between devices, swap(): return lax.all_to_all(array, 'gy', split_axis=1, concat_axis=1, tiled=True)  23.2 us
    all_to_all x2, starting transfers between devices, swap(): return lax.all_to_all(array, 'gy', split_axis=1, concat_axis=1, tiled=True)  19.7 us
    all_to_all x2, waiting for transfers between devices, swap(): array = lax.all_to_all(array, 'gx', split_axis=0, concat_axis=0, tiled=True)  13 us
    unnamed x27, local copies, waits for them, and re-layouts  12.3 us
    all_to_all x2, starting transfers between devices, swap(): array = lax.all_to_all(array, 'gx', split_axis=0, concat_axis=0, tiled=True)  11.3 us
    scatter x1, local copies, waits for them, and re-layouts, observed_field(): jnp.full((devices_all * capacity,), -1, jnp.int32).at[slot_index]  8.23 us
  transfers between devices with their start and end apart: 4, of which 2 were waited for; matrix products, arithmetic and copies ran while one was open for 12% of the time, Pallas kernels for 0%

profile of v1, /device:TPU:1, one launch (start us, length us, event | category | flops | bytes accessed | tf_op | source)
XLA Modules:
  0.0 225.5 jit_solution(1544221987873909150)
XLA Ops:
  1.5 1.2 copy.31
  2.8 0.9 fusion
  3.7 8.2 %scatter_custom_fusion = s32[4096]{0:T(1024)S(1)} fusion(s32[2048]{0:T(1024)S(1)} %bitcast.46, s32[2048]{0:T(1024)} %param.17, s32[]{:T(128)} %constant.12.clone.1), kind=kCustom, calls=%fused_computation.21 | custom fusion | bytes 16896 | tf_op jit(solution)/shard_map/scatter | solution.py:299
  12.8 6.5 %all-to-all-start = ((s32[8,1,512]{2,1,0:T(1,128)}), s32[8,1,512]{2,1,0:T(1,128)S(1)}, u32[]{:S(2)}, u32[]{:S(2)}) async-start(s32[8,1,512]{2,1,0:T(1,128)} %reshape.108), calls=%async_computation | async-start | bytes 32768 | tf_op jit(solution)/shard_map/all_to_all | solution.py:304
  19.3 2.8 %fusion.10 = f32[2048,64]{1,0:T(8,128)} fusion(f32[2048,64]{0,1:T(8,128)S(1)} %copy-done, f32[64,64]{1,0:T(8,128)S(1)} %copy-done.7), kind=kOutput, calls=%fused_computation.25 | convolution fusion | flops 100663296 | bytes 1064960 | tf_op jit(solution)/shard_map/dot_general | solution.py:297
  22.1 6.5 %scatter_custom_fusion.1 = f32[4096,64]{1,0:T(8,128)S(1)} fusion(s32[2048]{0:T(1024)S(1)} %bitcast.47, f32[2048,64]{1,0:T(8,128)} %fusion.10, f32[]{:T(128)} %constant.11.clone.1), kind=kCustom, calls=%fused_computation.15 | custom fusion | bytes 1049088 | tf_op jit(solution)/shard_map/scatter | solution.py:298
  28.6 2.1 reshape.112
  30.7 4.8 %all-to-all-start.2 = ((f32[8,1,32768]{2,1,0:T(1,128)}), f32[8,1,32768]{2,1,0:T(1,128)S(1)}, u32[]{:S(2)}, u32[]{:S(2)}) async-start(f32[8,1,32768]{2,1,0:T(1,128)} %reshape.112), calls=%async_computation.2 | async-start | bytes 2097152 | tf_op jit(solution)/shard_map/all_to_all | solution.py:304
  37.6 13.0 %all-to-all-done.2 = f32[8,1,32768]{2,1,0:T(1,128)S(1)} async-done(((f32[8,1,32768]{2,1,0:T(1,128)}), f32[8,1,32768]{2,1,0:T(1,128)S(1)}, u32[]{:S(2)}, u32[]{:S(2)}) %all-to-all-start.2) | async-done | bytes 1048608 | tf_op jit(solution)/shard_map/all_to_all | solution.py:304
  50.6 10.7 %all-to-all-start.1 = ((s32[32,1,128]{2,1,0:T(1,128)}), s32[32,1,128]{2,1,0:T(1,128)S(1)}, u32[]{:S(2)}, u32[]{:S(2)}) async-start(s32[32,1,128]{2,1,0:T(1,128)} %reshape.110), calls=%async_computation.1 | async-start | bytes 32768 | tf_op jit(solution)/shard_map/all_to_all | solution.py:305
  61.8 4.5 %reduce.2 = f32[8,32768]{1,0:T(8,128)} reduce(f32[8,1,32768]{2,1,0:T(1,128)S(1)} %all-to-all-done.2, f32[]{:T(128)} %broadcast.75), dimensions={1}, to_apply=%all_to_all.14.reduce_sub_computation | reduce | bytes 2097156 | tf_op jit(solution)/shard_map/all_to_all | solution.py:304
  66.3 2.1 reshape.113
  68.4 1.6 copy.43
  70.0 3.4 %reshape.114 = f32[32,1,8192]{2,1,0:T(1,128)} reshape(f32[32,8,16,64]{3,2,1,0:T(8,128)} %bitcast.35) | data formatting | bytes 2097152
  73.4 9.1 %all-to-all-start.3 = ((f32[32,1,8192]{2,1,0:T(1,128)}), f32[32,1,8192]{2,1,0:T(1,128)S(1)}, u32[]{:S(2)}, u32[]{:S(2)}) async-start(f32[32,1,8192]{2,1,0:T(1,128)} %reshape.114), calls=%async_computation.3 | async-start | bytes 2097152 | tf_op jit(solution)/shard_map/all_to_all | solution.py:305
  83.8 23.2 %all-to-all-done.3 = f32[32,1,8192]{2,1,0:T(1,128)S(1)} async-done(((f32[32,1,8192]{2,1,0:T(1,128)}), f32[32,1,8192]{2,1,0:T(1,128)S(1)}, u32[]{:S(2)}, u32[]{:S(2)}) %all-to-all-start.3) | async-done | bytes 1048608 | tf_op jit(solution)/shard_map/all_to_all | solution.py:305
  107.0 4.4 %reduce.3 = f32[32,8192]{1,0:T(8,128)} reduce(f32[32,1,8192]{2,1,0:T(1,128)S(1)} %all-to-all-done.3, f32[]{:T(128)} %broadcast.75), dimensions={1}, to_apply=%all_to_all.15.reduce_sub_computation | reduce | bytes 2097156 | tf_op jit(solution)/shard_map/all_to_all | solution.py:305
  111.4 2.0 reshape.115
  113.6 3.2 %bitcast_select_fusion.1 = f32[4096,64]{1,0:T(8,128)} fusion(f32[8,32,16,64]{3,2,1,0:T(8,128)S(1)} %copy.39, pred[4096]{0:T(1024)(128)(4,1)S(1)} %ge.27), kind=kLoop, calls=%fused_computation.5 | loop fusion | flops 262144 | bytes 2101248 | tf_op jit(solution)/shard_map/jit(_where)/select_n | solution.py:311
  116.8 23.7 %scatter_custom_fusion.2 = f32[4096,64]{1,0:T(8,128)S(1)} fusion(s32[4096]{0:T(1024)S(1)} %bitcast.45, f32[4096,64]{1,0:T(8,128)} %bitcast_select_fusion.1, f32[]{:T(128)} %constant.11.clone.1), kind=kCustom, calls=%fused_computation.13 | custom fusion | flops 262144 | bytes 1049088 | tf_op jit(solution)/shard_map/scatter-add | solution.py:310
  140.5 1.8 copy.40
  142.3 1.9 bitcast_add_fusion
  144.5 80.0 %field_solve.1 = f32[2048,128]{1,0:T(8,128)S(1)} custom-call(f32[2048,128]{1,0:T(8,128)S(1)} %bitcast.31, f32[64,64]{1,0:T(8,128)S(1)} %copy-done.2, f32[64,64]{1,0:T(8,128)S(1)} %copy-done.3, f32[64]{0:T(128)S(1)} %copy-done.5, bf16[1024,1024]{1,0:T(8,128)(2,1)S(1)} %copy-done.1, bf16[1024,1024]{1,0:T(8,128)(2,1)} %constant.32.clone.c_lo, ...), custom_call_target="tpu_custom_call" | custom-call | tf_op jit(solution)/shard_map/field_solve/pallas_call | solution.py:252
  224.5 1.0 copy.45
  (48 shorter events, 6.7 us)
Async XLA Ops:
  0.0 19.3 %copy-start = (f32[2048,64]{0,1:T(8,128)S(1)}, f32[2048,64]{0,1:T(8,128)}, u32[]{:S(2)}) copy-start(f32[2048,64]{0,1:T(8,128)} %param.15) | copy-start | bytes 1572868
  1.5 1.3 copy-start.6
  2.7 16.6 %copy-start.7 = (f32[64,64]{1,0:T(8,128)S(1)}, f32[64,64]{1,0:T(8,128)}, u32[]{:S(2)}) copy-start(f32[64,64]{1,0:T(8,128)} %param.18) | copy-start | bytes 49156
  12.8 17.9 %all-to-all-start = ((s32[8,1,512]{2,1,0:T(1,128)}), s32[8,1,512]{2,1,0:T(1,128)S(1)}, u32[]{:S(2)}, u32[]{:S(2)}) async-start(s32[8,1,512]{2,1,0:T(1,128)} %reshape.108), calls=%async_computation | async-start | bytes 32768 | tf_op jit(solution)/shard_map/all_to_all | solution.py:304
  30.7 19.9 %all-to-all-start.2 = ((f32[8,1,32768]{2,1,0:T(1,128)}), f32[8,1,32768]{2,1,0:T(1,128)S(1)}, u32[]{:S(2)}, u32[]{:S(2)}) async-start(f32[8,1,32768]{2,1,0:T(1,128)} %reshape.112), calls=%async_computation.2 | async-start | bytes 2097152 | tf_op jit(solution)/shard_map/all_to_all | solution.py:304
  50.6 22.8 %all-to-all-start.1 = ((s32[32,1,128]{2,1,0:T(1,128)}), s32[32,1,128]{2,1,0:T(1,128)S(1)}, u32[]{:S(2)}, u32[]{:S(2)}) async-start(s32[32,1,128]{2,1,0:T(1,128)} %reshape.110), calls=%async_computation.1 | async-start | bytes 32768 | tf_op jit(solution)/shard_map/all_to_all | solution.py:305
  73.4 33.6 %all-to-all-start.3 = ((f32[32,1,8192]{2,1,0:T(1,128)}), f32[32,1,8192]{2,1,0:T(1,128)S(1)}, u32[]{:S(2)}, u32[]{:S(2)}) async-start(f32[32,1,8192]{2,1,0:T(1,128)} %reshape.114), calls=%async_computation.3 | async-start | bytes 2097152 | tf_op jit(solution)/shard_map/all_to_all | solution.py:305
  142.2 1.9 copy-start.8
  142.2 2.2 copy-start.1
  142.2 2.2 copy-start.2
  142.2 2.2 copy-start.3
  142.2 2.2 copy-start.4
  142.2 2.2 copy-start.5

commit v2 on v1

--- a/solution.py
+++ b/solution.py
@@ -15,6 +15,9 @@
 LANES = 128
 Y_CUTS = 2
 K_CUTS = 2
+R_CUTS = 3
+R_PLANES = 3
+TILE = 256
 
 
 def wave_order(length):
@@ -46,13 +49,23 @@
     return jnp.dot(left, right, preferred_element_type=F32)
 
 
+def dot_nt(left, right):
+    return lax.dot_general(left, right, (((1,), (1,)), ((), ())), preferred_element_type=F32)
+
+
 def wait_for(ref, sem):
     pltpu.make_async_copy(ref, ref, sem).wait()
 
 
 def field_kernel(
-    n_gx, n_gy, gy_dims, field, vinv, vbas, eigen, c_hi, c_lo, t_hi, t_lo, line_col, line_row, out,
+    n_gx, n_gy, gy_dims,
+    field_hbm, innov, owner, column, weight, vinv, vbas, eigen,
+    c_hi_hbm, c_lo_hbm, t_hi_hbm, t_lo_hbm, line_col_hbm, line_row,
+    out,
+    field, c_hi, c_lo, t_hi, t_lo, line_col,
+    hots, expanded, slots, relay, relay_out, got, sums,
     vert, x_in, x_out, y_in, y_out, z_in, z_out, phys, solved,
+    load_sem, rx_send, rx_recv, ry_send, ry_recv,
     xf_send, xf_recv, yf_send, yf_recv, yb_send, yb_recv, xb_send, xb_recv,
 ):
     gx = lax.axis_index("gx")
@@ -73,6 +86,18 @@
         low = lax.rem(gy + step, n_lo)
         return high * n_lo + low
 
+    loads = [
+        pltpu.make_async_copy(source, target, load_sem.at[i])
+        for i, (source, target) in enumerate(
+            [
+                (field_hbm, field), (t_hi_hbm, t_hi), (t_lo_hbm, t_lo), (c_hi_hbm, c_hi),
+                (c_lo_hbm, c_lo), (line_col_hbm, line_col),
+            ]
+        )
+    ]
+    for load in loads:
+        load.start()
+
     barrier = pltpu.get_barrier_semaphore()
 
     def greet_gx(step, carry):
@@ -129,16 +154,160 @@
 
     vert3 = vert.reshape(levels, rows_y, LANES)
     phys3 = phys.reshape(levels, rows_y, LANES)
-
+    devices = n_gx * n_gy
+    slot_pairs = R_CUTS * R_PLANES - 1
+    chunks = owner.shape[0]
+    side = lax.broadcasted_iota(jnp.int32, (devices, TILE), 0)
+
+    def number_rows():
+        before = jnp.where(
+            lax.broadcasted_iota(jnp.int32, (TILE, TILE), 0)
+            < lax.broadcasted_iota(jnp.int32, (TILE, TILE), 1),
+            1.0, 0.0,
+        ).astype(BF16)
+        seen = jnp.zeros((devices, 1), F32)
+        ranks = []
+        for chunk in range(chunks):
+            hot = jnp.where(side == owner[chunk : chunk + 1, :], 1.0, 0.0)
+            narrow = hot.astype(BF16)
+            hots[:, chunk * TILE : (chunk + 1) * TILE] = narrow
+            earlier = dot(narrow, before) + seen
+            ranks.append(jnp.sum(hot * earlier, axis=0, keepdims=True).astype(jnp.int32))
+            seen = seen + jnp.sum(hot, axis=1, keepdims=True)
+        return ranks
+
+    def weigh_rows(ranks):
+        mixed = lax.dot_general(
+            weight[...], vinv[...], (((1,), (1,)), ((), ())),
+            precision=lax.Precision.HIGHEST, preferred_element_type=F32,
+        )
+        w_hi, w_lo = halves(jnp.concatenate([mixed, mixed], axis=1))
+        upper = lax.broadcasted_iota(jnp.int32, (LANES, LANES), 1) >= levels
+        for chunk in range(chunks):
+            rows = slice(chunk * TILE, (chunk + 1) * TILE)
+            hi, lo = halves(innov[rows, :])
+            rows_m = dot(hi, w_hi) + dot(lo, w_hi) + dot(hi, w_lo)
+            odd = (ranks[chunk] & 1).astype(F32)
+            keep = []
+            for i in range(TILE // LANES):
+                turned = jnp.broadcast_to(odd[:, i * LANES : (i + 1) * LANES], (LANES, LANES)).T
+                keep.append(jnp.where(upper, turned, 1.0 - turned))
+            hi, lo = halves(rows_m * jnp.concatenate(keep, axis=0))
+            expanded[rows, :LANES] = hi
+            expanded[rows, LANES:] = lo
+
+    def place_codes(ranks):
+        wide_side = lax.broadcasted_iota(jnp.int32, (LANES, TILE), 0)
+        high = jnp.zeros((devices, LANES), F32)
+        low = jnp.zeros((devices, LANES), F32)
+        for chunk in range(chunks):
+            lane = (ranks[chunk] & 1) * slot_pairs + (ranks[chunk] >> 1)
+            code = column[chunk : chunk + 1, :] + 1
+            here = wide_side == lane
+            hot = hots[:, chunk * TILE : (chunk + 1) * TILE]
+            high += dot_nt(hot, jnp.where(here, (code >> 6).astype(F32), 0.0).astype(BF16))
+            low += dot_nt(hot, jnp.where(here, (code & 63).astype(F32), 0.0).astype(BF16))
+        slots[0] = high * 64.0 + low
+
+    def place_rows(ranks, pair):
+        total = jnp.zeros((devices, TILE), F32)
+        for chunk in range(chunks):
+            mask = jnp.where((ranks[chunk] >> 1) == pair, 1.0, 0.0).astype(BF16)
+            hot = hots[:, chunk * TILE : (chunk + 1) * TILE] * mask
+            total += dot(hot, expanded[chunk * TILE : (chunk + 1) * TILE, :])
+        slots[pair + 1] = total[:, :LANES] + total[:, LANES:]
+
+    ranks = number_rows()
+    place_codes(ranks)
+    weigh_rows(ranks)
+    for r in range(R_CUTS):
+        planes = pl.ds(r * R_PLANES, R_PLANES)
+        for plane in range(r * R_PLANES, (r + 1) * R_PLANES):
+            if plane > 0:
+                place_rows(ranks, plane - 1)
+        if r == 0:
+            pl.semaphore_wait(barrier, n_gx - 1 + n_gy - 1)
+        send_gx(
+            lambda a: slots.at[planes, pl.ds(a * n_gy, n_gy), :],
+            relay.at[planes, gx, :, :],
+            rx_send.at[r], rx_recv.at[r],
+        )
+
+    def pass_on(r):
+        wait_for(relay.at[pl.ds(r * R_PLANES, R_PLANES)], rx_recv.at[r])
+        for i in range(R_PLANES):
+            plane = relay.at[r * R_PLANES + i].reshape(devices, LANES)
+            for b in range(n_gy):
+                relay_out[r, b, i, :, :] = plane[pl.ds(b, n_gx, stride=n_gy), :]
+        send_gy(
+            lambda b: relay_out.at[r, b], got.at[r, gy], ry_send.at[r], ry_recv.at[r]
+        )
+
+    pass_on(0)
+    loads[0].wait()
     for h in range(Y_CUTS):
         mix_levels(vinv[...], field, vert, h)
-        if h == 0:
-            pl.semaphore_wait(barrier, n_gx - 1 + n_gy - 1)
+    for r in range(1, R_CUTS):
+        pass_on(r)
+
+    spots = 4
+    area = rows_y * LANES // spots
+    place_side = lax.broadcasted_iota(jnp.int32, (area, devices), 0)
+
+    def add_rows(r, codes):
+        lefts, rights = [], []
+        for i in range(R_PLANES):
+            pair = r * R_PLANES + i - 1
+            if pair < 0:
+                continue
+            data = got[r, :, i, :, :].reshape(devices, LANES).T
+            hi, lo = halves(data)
+            for half in range(2):
+                code = codes[half * slot_pairs + pair : half * slot_pairs + pair + 1, :]
+                spot, place = code >> 10, code & (area - 1)
+                both = jnp.concatenate(
+                    [part[half * levels : (half + 1) * levels, :] for part in (hi, lo)], axis=0
+                )
+                lefts.append(
+                    jnp.concatenate(
+                        [
+                            both * jnp.where(spot == s, 1.0, 0.0).astype(BF16)
+                            for s in range(spots)
+                        ],
+                        axis=0,
+                    )
+                )
+                rights.append(jnp.where(place_side == place, 1.0, 0.0).astype(BF16))
+        term = dot_nt(jnp.concatenate(lefts, axis=1), jnp.concatenate(rights, axis=1))
+        if r == 0:
+            sums[...] = term
+        else:
+            sums[...] += term
+
+    codes = None
+    for r in range(R_CUTS):
+        wait_for(got.at[r], ry_recv.at[r])
+        if r == 0:
+            codes = got[0, :, 0, :, :].reshape(devices, LANES).T.astype(jnp.int32) - 1
+        add_rows(r, codes)
+
+    per_spot = rows_y // spots
+    for h in range(Y_CUTS):
+        for y in range(h * cut, (h + 1) * cut):
+            spot, lanes = y // per_spot, slice((y % per_spot) * LANES, (y % per_spot + 1) * LANES)
+            top = spot * 2 * levels
+            rows = pl.ds(y, levels, stride=rows_y)
+            vert[rows, :] = (
+                vert[rows, :] + sums[top : top + levels, lanes]
+                + sums[top + levels : top + 2 * levels, lanes]
+            )
         send_gx(
             lambda a: vert3.at[pl.ds(a * own_levels, own_levels), y_span(h), :],
             x_in.at[gx, :, y_span(h), :],
             xf_send.at[h], xf_recv.at[h],
         )
+    for load in loads[1:]:
+        load.wait()
 
     wide = 2 * LANES
 
@@ -228,6 +397,9 @@
         wait_for(phys3.at[:, y_span(h), :], xb_recv.at[h])
         mix_levels(vbas[...], phys, out, h)
 
+    for r in range(R_CUTS):
+        wait_for(relay.at[pl.ds(r * R_PLANES, R_PLANES), pl.ds(0, n_gx - 1)], rx_send.at[r])
+        wait_for(got.at[r, pl.ds(0, n_gy - 1)], ry_send.at[r])
     for h in range(Y_CUTS):
         wait_for(x_in.at[pl.ds(0, n_gx - 1), :, y_span(h), :], xf_send.at[h])
         wait_for(z_out.at[pl.ds(0, n_gx - 1), :, y_span(h), :], xb_send.at[h])
@@ -236,25 +408,44 @@
             wait_for(y_out.at[k, pl.ds(0, n_gy - 1), y_span(h), :], yb_send.at[k, h])
 
 
-def solve_field(forcing_total, vert_inverse, vert_basis, vert_eigen, gy_dims):
+def per_device(
+    forcing_field, innovations, owner_device, column_index, obs_weight, vert_inverse, vert_basis,
+    vert_eigen,
+):
     n_gx = lax.axis_size("gx")
     n_gy = lax.axis_size("gy")
-    levels, rows_y, cols_x = forcing_total.shape
+    devices = n_gx * n_gy
+    levels, rows_y, cols_x = forcing_field.shape
     length = cols_x * n_gx
     (c_hi, c_lo), (t_hi, t_lo), line = wave_tables(length)
     own_levels = levels // n_gx
     parts = n_gy // own_levels
+    planes = R_CUTS * R_PLANES
     line_col = np.broadcast_to(line[:, None], (length, LANES))
     line_row = line.reshape(K_CUTS * parts, LANES)
     vmem = pl.BlockSpec(memory_space=pltpu.VMEM)
     smem = pl.BlockSpec(memory_space=pltpu.SMEM)
+    hbm = pl.BlockSpec(memory_space=pl.ANY)
     dma = pltpu.SemaphoreType.DMA
     out = pl.pallas_call(
-        functools.partial(field_kernel, n_gx, n_gy, gy_dims),
+        functools.partial(field_kernel, n_gx, n_gy, (4, 8)),
         out_shape=jax.ShapeDtypeStruct((levels * rows_y, cols_x), F32),
-        in_specs=[vmem, vmem, vmem, smem, vmem, vmem, vmem, vmem, vmem, vmem],
+        in_specs=[hbm, vmem, vmem, vmem, vmem, vmem, vmem, smem, hbm, hbm, hbm, hbm, hbm, vmem],
         out_specs=vmem,
         scratch_shapes=[
+            pltpu.VMEM((levels * rows_y, LANES), F32),
+            pltpu.VMEM((length, length), BF16),
+            pltpu.VMEM((length, length), BF16),
+            pltpu.VMEM((length, length), BF16),
+            pltpu.VMEM((length, length), BF16),
+            pltpu.VMEM((length, LANES), F32),
+            pltpu.VMEM((devices, innovations.shape[0]), BF16),
+            pltpu.VMEM((innovations.shape[0], 2 * LANES), BF16),
+            pltpu.VMEM((planes, devices, LANES), F32),
+            pltpu.VMEM((planes, n_gx, n_gy, LANES), F32),
+            pltpu.VMEM((R_CUTS, n_gy, R_PLANES, n_gx, LANES), F32),
+            pltpu.VMEM((R_CUTS, n_gy, R_PLANES, n_gx, LANES), F32),
+            pltpu.VMEM((8 * levels, rows_y * cols_x // 4), F32),
             pltpu.VMEM((levels * rows_y, LANES), F32),
             pltpu.VMEM((n_gx, own_levels, rows_y, LANES), F32),
             pltpu.VMEM((K_CUTS, own_levels, parts, rows_y, LANES), F32),
@@ -264,65 +455,25 @@
             pltpu.VMEM((n_gx, own_levels, rows_y, LANES), F32),
             pltpu.VMEM((levels * rows_y, LANES), F32),
             pltpu.VMEM((length, 2 * LANES), BF16),
+            dma((6,)),
+            dma((R_CUTS,)), dma((R_CUTS,)),
+            dma((R_CUTS,)), dma((R_CUTS,)),
             dma((Y_CUTS,)), dma((Y_CUTS,)),
             dma((K_CUTS, Y_CUTS)), dma((K_CUTS, Y_CUTS)),
             dma((K_CUTS, Y_CUTS)), dma((K_CUTS, Y_CUTS)),
             dma((Y_CUTS,)), dma((Y_CUTS,)),
         ],
         compiler_params=pltpu.CompilerParams(
-            collective_id=0, has_side_effects=True, vmem_limit_bytes=48 * 1024 * 1024
+            collective_id=0, has_side_effects=True, vmem_limit_bytes=56 * 1024 * 1024
         ),
         name="field_solve",
     )(
-        forcing_total.reshape(levels * rows_y, cols_x), vert_inverse, vert_basis, vert_eigen,
+        forcing_field.reshape(levels * rows_y, cols_x), innovations,
+        owner_device.reshape(-1, TILE), column_index.reshape(-1, TILE), obs_weight,
+        vert_inverse, vert_basis, vert_eigen,
         c_hi, c_lo, t_hi, t_lo, line_col, line_row,
     )
     return out.reshape(levels, rows_y, cols_x)
-
-
-def observed_field(innovations, owner_device, column_index, obs_weight, shape):
-    highest = lax.Precision.HIGHEST
-    levels, cols_y, cols_x = shape
-    groups_x = lax.axis_size("gx")
-    groups_y = lax.axis_size("gy")
-    devices_all = groups_x * groups_y
-    row_total = innovations.shape[0]
-    capacity = 2 * row_total // devices_all
-    targets = owner_device[:, 0]
-    one_hot = (targets[:, None] == jnp.arange(devices_all, dtype=jnp.int32)[None, :]).astype(
-        jnp.int32
-    )
-    rank_in_peer = jnp.sum(jnp.cumsum(one_hot, axis=0) * one_hot, axis=1) - 1
-    slot_index = targets * capacity + rank_in_peer
-    payload = jnp.dot(innovations, obs_weight, precision=highest, preferred_element_type=F32)
-    send_rows = jnp.zeros((devices_all * capacity, levels), F32).at[slot_index].set(payload)
-    send_cols = jnp.full((devices_all * capacity,), -1, jnp.int32).at[slot_index].set(column_index)
-    send_rows = send_rows.reshape(groups_x, groups_y, capacity, levels)
-    send_cols = send_cols.reshape(groups_x, groups_y, capacity)
-
-    def swap(array):
-        array = lax.all_to_all(array, "gx", split_axis=0, concat_axis=0, tiled=True)
-        return lax.all_to_all(array, "gy", split_axis=1, concat_axis=1, tiled=True)
-
-    flat_rows = swap(send_rows).reshape(devices_all * capacity, levels)
-    flat_cols = swap(send_cols).reshape(devices_all * capacity)
-    row_valid = flat_cols >= 0
-    summed = jax.ops.segment_sum(
-        jnp.where(row_valid[:, None], flat_rows, 0.0),
-        jnp.where(row_valid, flat_cols, 0),
-        num_segments=cols_y * cols_x,
-    )
-    return summed.reshape(cols_y, cols_x, levels).transpose(2, 0, 1)
-
-
-def per_device(
-    forcing_field, innovations, owner_device, column_index, obs_weight, vert_inverse, vert_basis,
-    vert_eigen,
-):
-    observed = observed_field(
-        innovations, owner_device, column_index, obs_weight, forcing_field.shape
-    )
-    return solve_field(forcing_field + observed, vert_inverse, vert_basis, vert_eigen, (4, 8))
 
 
 def solution(mesh):

time: 226 us -> 132 us (0.58)
  Pallas kernels: 80 us -> 121 us
  other arithmetic: 40.4 us -> 1.36 us
  waiting for transfers between devices: 36.2 us -> 0 us
  starting transfers between devices: 31 us -> 0 us
  local copies, waits for them, and re-layouts: 34.7 us -> 8.72 us
  matrix products: 2.78 us -> 0 us
    pallas_call x1, Pallas kernels: 80 us -> 121 us  [per_device(): pl.pallas_call(functools.partial(field_kernel, n_gx, n_gy, (4, 8)), out_s...]
    all_to_all x4 -> x0, waiting for transfers between devices: 36.2 us -> none  [the longest x2 23.2 us: swap(): return lax.all_to_all(array, 'gy', split_axis=1, concat_axis=1, tiled=True)]
    all_to_all x4 -> x0, starting transfers between devices: 31 us -> none  [the longest x2 19.7 us: swap(): return lax.all_to_all(array, 'gy', split_axis=1, concat_axis=1, tiled=True)]
    scatter-add x1 -> x0, other arithmetic: 23.7 us -> none  [observed_field(): jax.ops.segment_sum(jnp.where(row_valid[:, None], flat_rows, 0.0), jnp.wh...]
    scatter x2 -> x0, local copies, waits for them, and re-layouts: 14.7 us -> none  [the longest x1 8.23 us: observed_field(): jnp.full((devices_all * capacity,), -1, jnp.int32).at[slot_index]]
    all_to_all x4 -> x0, other arithmetic: 10.1 us -> none  [the longest x2 5.12 us: swap(): array = lax.all_to_all(array, 'gx', split_axis=0, concat_axis=0, tiled=True)]
    unnamed x27 -> x3, local copies, waits for them, and re-layouts: 12.3 us -> 5.12 us
    select_n x3 -> x0, other arithmetic: 3.21 us -> none  [the longest x1 3.17 us: observed_field(): jnp.where(row_valid[:, None], flat_rows, 0.0)]
  transfers between devices with their start and end apart: 4 -> 0, of which waited for: 2 -> 0; matrix products, arithmetic and copies ran while one was open for 12% -> 0% of each run, Pallas kernels for 0% -> 0%
where the time goes in v2:
time: 132 us; the launch traced here: 131 us
  Pallas kernels  121 us (92%)
  local copies, waits for them, and re-layouts  8.72 us (7%)
  other arithmetic  1.36 us (1%)
    pallas_call x1, Pallas kernels, per_device(): pl.pallas_call(functools.partial(field_kernel, n_gx, n_gy, (4, 8)), out_s...  121 us
    unnamed x3, local copies, waits for them, and re-layouts  5.12 us

profile of v2, /device:TPU:1, one launch (start us, length us, event | category | flops | bytes accessed | tf_op | source)
XLA Modules:
  0.0 131.3 jit_solution(11556286893115595751)
XLA Ops:
  0.0 0.5 broadcast.3
  0.5 1.4 %reduce.3 = s32[2048]{0:T(1024)S(1)} reduce(s32[2048,1]{0,1:T(1,128)} %param.16, s32[]{:T(128)} %broadcast.3), dimensions={1}, to_apply=%param.16.reduce_sub_computation.3 | reduce | bytes 16388 | tf_op args[2]
  1.9 0.6 reshape.13.owner
  2.5 1.3 reshape.14.column
  3.8 2.4 %copy.15.innov = f32[2048,64]{1,0:T(8,128)} copy(f32[2048,64]{0,1:T(8,128)} %param.15) | data formatting | bytes 1048576 | tf_op args[1]
  6.1 1.7 %jit_solution_.3.line_col_hbm = f32[1024,128]{1,0:T(8,128)} broadcast(f32[1024]{0:T(1024)} %constant.16.clone), dimensions={0} | broadcast | bytes 528384 | tf_op jit(solution)
  7.8 121.2 %field_solve.1 = f32[2048,128]{1,0:T(8,128)} custom-call(f32[2048,128]{1,0:T(8,128)} %bitcast.4, f32[2048,64]{1,0:T(8,128)} %copy.15.innov, s32[8,256]{1,0:T(8,128)} %reshape.13.owner, s32[8,256]{1,0:T(8,128)} %reshape.14.column, f32[64,64]{1,0:T(8,128)} %weight.1, f32[64,64]{1,0:T(8,128)} %vinv.1, f32[64,64]{1,0:T(8,128)} %vbas.1, f32[64]{0:T(128)} %eigen.1, ...), custom_call_target="tpu_custom_call" | custom-call | tf_op jit(solution)/shard_map/field_solve/pallas_call | solution.py:430
  129.0 2.3 %copy.17 = f32[64,32,128]{2,1,0:T(8,128)} copy(f32[64,32,128]{2,1,0:T(8,128)} %bitcast.3) | data formatting | bytes 2097152

commit v3 on v2

v3 whole, which is shorter than its diff:
```python
import functools

import jax
import jax.numpy as jnp
import ml_dtypes
import numpy as np
from jax import lax
from jax.experimental import pallas as pl
from jax.experimental.pallas import tpu as pltpu
from jax.sharding import PartitionSpec as P

MESH = pl.DeviceIdType.MESH
F32 = jnp.float32
BF16 = jnp.bfloat16
LANES = 128
Y_CUTS = 2
R_CUTS = 3
R_PLANES = 3
TILE = 256


def split_table(table):
    high = table.astype(np.float32).astype(ml_dtypes.bfloat16)
    low = (table - high.astype(np.float64)).astype(np.float32).astype(ml_dtypes.bfloat16)
    return high, low


def wave_tables(length):
    waves = np.arange(length, dtype=np.float64)
    scales = np.where(waves == 0, np.sqrt(1.0 / length), np.sqrt(2.0 / length))
    table = scales[:, None] * np.cos(np.pi * waves[:, None] * (2 * waves + 1) / (2 * length))
    line = 4.0 * np.sin(np.pi * waves / (2.0 * length)) ** 2
    return split_table(table), split_table(table.T), line.astype(np.float32)


def halves(value):
    high = value.astype(BF16)
    low = (value - high.astype(F32)).astype(BF16)
    return high, low


def dot(left, right):
    return jnp.dot(left, right, preferred_element_type=F32)


def dot_nt(left, right):
    return lax.dot_general(left, right, (((1,), (1,)), ((), ())), preferred_element_type=F32)


def wait_for(ref, sem):
    pltpu.make_async_copy(ref, ref, sem).wait()


def power(value, doublings):
    for _ in range(doublings):
        value = value * value
    return value


def decay(sigma):
    root = jnp.sqrt(sigma + 0.25 * sigma * sigma)
    return 1.0 / (1.0 + 0.5 * sigma + root), 0.5 / root


def field_kernel(
    n_gx, n_gy, gy_dims,
    field_hbm, innov, owner, column, weight, vinv, vbas, eigen,
    t_hi_hbm, t_lo_hbm, c_hi_hbm, c_lo_hbm, line,
    out,
    field, t_hi, t_lo, c_hi, c_lo,
    hots, expanded, slots, relay, relay_out, got, sums,
    vert, x_in, spec, run, edge_out, edge_in, inflow_out, inflow_in, inflow, z_out, phys,
    load_sem, rx_send, rx_recv, ry_send, ry_recv,
    xf_send, xf_recv, edge_send, edge_recv, flow_send, flow_recv, xb_send, xb_recv,
):
    gx = lax.axis_index("gx")
    gy = lax.axis_index("gy")
    n_hi, n_lo = gy_dims
    rows_y, levels, _ = vert.shape
    own_levels = levels // n_gx
    cut = rows_y // Y_CUTS
    length = t_hi.shape[0]

    def gx_peer(step):
        return lax.rem(gx + step, n_gx)

    def gy_peer(step):
        high = lax.rem(gy // n_lo + step // n_lo, n_hi)
        low = lax.rem(gy + step, n_lo)
        return high * n_lo + low

    loads = [
        pltpu.make_async_copy(source, target, load_sem.at[i])
        for i, (source, target) in enumerate(
            [
                (field_hbm, field), (t_hi_hbm, t_hi), (t_lo_hbm, t_lo), (c_hi_hbm, c_hi),
                (c_lo_hbm, c_lo),
            ]
        )
    ]
    for load in loads:
        load.start()

    barrier = pltpu.get_barrier_semaphore()

    def greet_gx(step, carry):
        pl.semaphore_signal(barrier, inc=1, device_id=(gx_peer(step), gy), device_id_type=MESH)
        return carry

    def greet_gy(step, carry):
        pl.semaphore_signal(barrier, inc=1, device_id=(gx, gy_peer(step)), device_id_type=MESH)
        return carry

    lax.fori_loop(1, n_gx, greet_gx, 0)
    lax.fori_loop(1, n_gy, greet_gy, 0)

    def mix_levels(matrix, read, write, y_cut):
        m_hi, m_lo = halves(matrix)
        stack = jnp.concatenate([m_hi, m_hi, m_lo], axis=1)
        for y in range(y_cut * cut, (y_cut + 1) * cut, 2):
            hi, lo = halves(jnp.concatenate([read(y), read(y + 1)], axis=1))
            mixed = dot(stack, jnp.concatenate([hi, lo, hi], axis=0))
            write(y, mixed[:, :LANES])
            write(y + 1, mixed[:, LANES:])

    def strided(ref, y):
        return ref.at[pl.ds(y, levels, stride=rows_y), :]

    def send_gx(source, target, send_sem, recv_sem):
        pltpu.make_async_copy(source(gx), target, recv_sem).start()

        def one(step, carry):
            peer = gx_peer(step)
            pltpu.make_async_remote_copy(
                src_ref=source(peer), dst_ref=target, send_sem=send_sem, recv_sem=recv_sem,
                device_id=(peer, gy), device_id_type=MESH,
            ).start()
            return carry

        lax.fori_loop(1, n_gx, one, 0)

    def send_gy(source, target, send_sem, recv_sem):
        pltpu.make_async_copy(source(gy), target, recv_sem).start()

        def one(step, carry):
            peer = gy_peer(step)
            pltpu.make_async_remote_copy(
                src_ref=source(peer), dst_ref=target, send_sem=send_sem, recv_sem=recv_sem,
                device_id=(gx, peer), device_id_type=MESH,
            ).start()
            return carry

        lax.fori_loop(1, n_gy, one, 0)

    def y_span(y_cut):
        return pl.ds(y_cut * cut, cut)

    devices = n_gx * n_gy
    slot_pairs = R_CUTS * R_PLANES - 1
    chunks = owner.shape[1] // TILE
    side = lax.broadcasted_iota(jnp.int32, (devices, TILE), 0)

    def number_rows():
        before = jnp.where(
            lax.broadcasted_iota(jnp.int32, (TILE, TILE), 0)
            < lax.broadcasted_iota(jnp.int32, (TILE, TILE), 1),
            1.0, 0.0,
        ).astype(BF16)
        seen = jnp.zeros((devices, 1), F32)
        ranks = []
        for chunk in range(chunks):
            hot = jnp.where(side == owner[:, chunk * TILE : (chunk + 1) * TILE], 1.0, 0.0)
            narrow = hot.astype(BF16)
            hots[:, chunk * TILE : (chunk + 1) * TILE] = narrow
            earlier = dot(narrow, before) + seen
            ranks.append(jnp.sum(hot * earlier, axis=0, keepdims=True).astype(jnp.int32))
            seen = seen + jnp.sum(hot, axis=1, keepdims=True)
        return ranks

    def weigh_rows(ranks):
        mixed = lax.dot_general(
            vinv[...], weight[...], (((1,), (1,)), ((), ())),
            precision=lax.Precision.HIGHEST, preferred_element_type=F32,
        )
        w_hi, w_lo = halves(jnp.concatenate([mixed, mixed], axis=0))
        stack = jnp.concatenate([w_hi, w_hi, w_lo], axis=1)
        upper = lax.broadcasted_iota(jnp.int32, (LANES, TILE), 0) // levels
        for chunk in range(chunks):
            lanes = slice(chunk * TILE, (chunk + 1) * TILE)
            hi, lo = halves(innov[:, lanes])
            rows_m = dot(stack, jnp.concatenate([hi, lo, hi], axis=0))
            hi, lo = halves(jnp.where(upper == (ranks[chunk] & 1), rows_m, 0.0))
            expanded[:LANES, lanes] = hi
            expanded[LANES:, lanes] = lo

    def place_codes(ranks):
        wide_side = lax.broadcasted_iota(jnp.int32, (LANES, TILE), 0)
        high = jnp.zeros((devices, LANES), F32)
        low = jnp.zeros((devices, LANES), F32)
        for chunk in range(chunks):
            lane = (ranks[chunk] & 1) * slot_pairs + (ranks[chunk] >> 1)
            code = column[:, chunk * TILE : (chunk + 1) * TILE] + 1
            here = wide_side == lane
            hot = hots[:, chunk * TILE : (chunk + 1) * TILE]
            high += dot_nt(hot, jnp.where(here, (code >> 6).astype(F32), 0.0).astype(BF16))
            low += dot_nt(hot, jnp.where(here, (code & 63).astype(F32), 0.0).astype(BF16))
        slots[0] = high * 64.0 + low

    def place_rows(ranks, pair):
        total = jnp.zeros((devices, TILE), F32)
        for chunk in range(chunks):
            mask = jnp.where((ranks[chunk] >> 1) == pair, 1.0, 0.0).astype(BF16)
            hot = hots[:, chunk * TILE : (chunk + 1) * TILE] * mask
            total += dot_nt(hot, expanded[:, chunk * TILE : (chunk + 1) * TILE])
        slots[pair + 1] = total[:, :LANES] + total[:, LANES:]

    ranks = number_rows()
    place_codes(ranks)
    weigh_rows(ranks)
    for r in range(R_CUTS):
        planes = pl.ds(r * R_PLANES, R_PLANES)
        for plane in range(r * R_PLANES, (r + 1) * R_PLANES):
            if plane > 0:
                place_rows(ranks, plane - 1)
        if r == 0:
            pl.semaphore_wait(barrier, n_gx - 1 + n_gy - 1)
        send_gx(
            lambda a: slots.at[planes, pl.ds(a * n_gy, n_gy), :],
            relay.at[planes, gx, :, :],
            rx_send.at[r], rx_recv.at[r],
        )

    def pass_on(r):
        wait_for(relay.at[pl.ds(r * R_PLANES, R_PLANES)], rx_recv.at[r])
        for i in range(R_PLANES):
            plane = relay.at[r * R_PLANES + i].reshape(devices, LANES)
            for b in range(n_gy):
                relay_out[r, b, i, :, :] = plane[pl.ds(b, n_gx, stride=n_gy), :]
        send_gy(
            lambda b: relay_out.at[r, b], got.at[r, gy], ry_send.at[r], ry_recv.at[r]
        )

    def set_vert(y, value):
        vert[y] = value

    pass_on(0)
    loads[0].wait()
    for h in range(Y_CUTS):
        mix_levels(vinv[...], lambda y: strided(field, y)[...], set_vert, h)
    for r in range(1, R_CUTS):
        pass_on(r)

    spots = 4
    area = rows_y * LANES // spots
    place_side = lax.broadcasted_iota(jnp.int32, (area, devices), 0)

    def add_rows(r, codes):
        lefts, rights = [], []
        for i in range(R_PLANES):
            pair = r * R_PLANES + i - 1
            if pair < 0:
                continue
            data = got[r, :, i, :, :].reshape(devices, LANES).T
            hi, lo = halves(data)
            for half in range(2):
                code = codes[half * slot_pairs + pair : half * slot_pairs + pair + 1, :]
                spot, place = code >> 10, code & (area - 1)
                both = jnp.concatenate(
                    [part[half * levels : (half + 1) * levels, :] for part in (hi, lo)], axis=0
                )
                lefts.append(
                    jnp.concatenate(
                        [
                            both * jnp.where(spot == s, 1.0, 0.0).astype(BF16)
                            for s in range(spots)
                        ],
                        axis=0,
                    )
                )
                rights.append(jnp.where(place_side == place, 1.0, 0.0).astype(BF16))
        term = dot_nt(jnp.concatenate(lefts, axis=1), jnp.concatenate(rights, axis=1))
        if r == 0:
            sums[...] = term
        else:
            sums[...] += term

    codes = None
    for r in range(R_CUTS):
        wait_for(got.at[r], ry_recv.at[r])
        if r == 0:
            codes = got[0, :, 0, :, :].reshape(devices, LANES).T.astype(jnp.int32) - 1
        add_rows(r, codes)

    per_spot = rows_y // spots
    for h in range(Y_CUTS):
        for y in range(h * cut, (h + 1) * cut):
            spot, lanes = y // per_spot, slice((y % per_spot) * LANES, (y % per_spot + 1) * LANES)
            top = spot * 2 * levels
            vert[y] = (
                vert[y] + sums[top : top + levels, lanes]
                + sums[top + levels : top + 2 * levels, lanes]
            )
        send_gx(
            lambda a: vert.at[y_span(h), pl.ds(a * own_levels, own_levels), :],
            x_in.at[gx, y_span(h)],
            xf_send.at[h], xf_recv.at[h],
        )
    for load in loads[1:]:
        load.wait()

    def times_table(lines, hi_table, lo_table, write):
        hi, lo = halves(lines)
        for block in range(length // TILE):
            cols = pl.ds(block * TILE, TILE)
            write(
                block,
                dot(hi, hi_table[:, cols]) + dot(lo, hi_table[:, cols]) + dot(hi, lo_table[:, cols]),
            )

    def level_sigma(first, count, waves):
        row = lax.broadcasted_iota(jnp.int32, (count, waves.shape[1]), 0)
        sigma = jnp.broadcast_to(waves, row.shape)
        for i in range(count):
            sigma = sigma + jnp.where(row == i, eigen[first + i], 0.0)
        return sigma

    ratio, scale = decay(level_sigma(gx * own_levels, own_levels, line[...]))

    def flat(ref, h):
        return ref[y_span(h)].reshape(cut * own_levels, length)

    ahead = jnp.zeros((own_levels, length), F32)
    for h in range(Y_CUTS):
        wait_for(x_in.at[:, y_span(h)], xf_recv.at[h])
        lines = jnp.concatenate(
            [x_in[a, y_span(h)].reshape(cut * own_levels, LANES) for a in range(n_gx)], axis=1
        )

        def set_spec(block, value):
            spec[y_span(h), :, block * TILE : (block + 1) * TILE] = value.reshape(
                cut, own_levels, TILE
            )

        times_table(lines, t_hi, t_lo, set_spec)
        for y in range(h * cut, (h + 1) * cut):
            ahead = spec[y] + ratio * ahead
            run[y] = ahead
    behind = jnp.zeros((own_levels, length), F32)
    for y in reversed(range(rows_y)):
        behind = ratio * behind
        run[y] += behind
        behind = spec[y] + behind

    groups = own_levels // 2
    for s in range(n_gy):
        top, lanes = s % groups * 2, slice(s // groups * LANES, (s // groups + 1) * LANES)
        edge_out[s, 0:2, :] = ahead[top : top + 2, lanes]
        edge_out[s, 2:4, :] = behind[top : top + 2, lanes]
    send_gy(lambda b: edge_out.at[b], edge_in.at[gy], edge_send, edge_recv)
    part = pl.ds(pl.multiple_of(gy // groups * LANES, LANES), LANES)
    one_ratio, _ = decay(
        level_sigma(gx * own_levels + lax.rem(gy, groups) * 2, 2, line[:, part])
    )
    hop = power(one_ratio, rows_y.bit_length() - 1)
    across = power(hop, n_gy.bit_length() - 1)
    wait_for(edge_in, edge_recv)
    right = jnp.zeros((2, LANES), F32)
    left = jnp.zeros((2, LANES), F32)
    for b in range(n_gy):
        right = edge_in[b, 0:2, :] + hop * right
        left = edge_in[n_gy - 1 - b, 2:4, :] + hop * left
    mirror = 1.0 / (1.0 - across * across)
    right, left = (left + across * right) * mirror, (right + across * left) * mirror
    for b in range(n_gy):
        inflow_out[b, 0:2, :] = right
        inflow_out[n_gy - 1 - b, 2:4, :] = left
        right = edge_in[b, 0:2, :] + hop * right
        left = edge_in[n_gy - 1 - b, 2:4, :] + hop * left
    send_gy(lambda b: inflow_out.at[b], inflow_in.at[gy], flow_send, flow_recv)
    wait_for(inflow_in, flow_recv)
    for s in range(n_gy):
        top, lanes = s % groups * 2, slice(s // groups * LANES, (s // groups + 1) * LANES)
        inflow[0, top : top + 2, lanes] = inflow_in[s, 0:2, :]
        inflow[1, top : top + 2, lanes] = inflow_in[s, 2:4, :]
    ahead = inflow[0]
    for y in range(rows_y):
        ahead = ratio * ahead
        run[y] += ahead
    behind = inflow[1]

    for h in reversed(range(Y_CUTS)):
        for y in reversed(range(h * cut, (h + 1) * cut)):
            behind = ratio * behind
            run[y] = (run[y] + behind) * scale

        def set_lines(block, value):
            for i in range(TILE // LANES):
                z_out[block * 2 + i, y_span(h)] = value[:, i * LANES : (i + 1) * LANES].reshape(
                    cut, own_levels, LANES
                )

        times_table(flat(run, h), c_hi, c_lo, set_lines)
        send_gx(
            lambda a: z_out.at[a, y_span(h)],
            phys.at[y_span(h), pl.ds(gx * own_levels, own_levels), :],
            xb_send.at[h], xb_recv.at[h],
        )

    def set_out(y, value):
        out[pl.ds(y, levels, stride=rows_y), :] = value

    for h in reversed(range(Y_CUTS)):
        wait_for(phys.at[y_span(h)], xb_recv.at[h])
        mix_levels(vbas[...], lambda y: phys[y], set_out, h)

    for r in range(R_CUTS):
        wait_for(relay.at[pl.ds(r * R_PLANES, R_PLANES), pl.ds(0, n_gx - 1)], rx_send.at[r])
        wait_for(got.at[r, pl.ds(0, n_gy - 1)], ry_send.at[r])
    for h in range(Y_CUTS):
        wait_for(x_in.at[pl.ds(0, n_gx - 1), y_span(h)], xf_send.at[h])
        wait_for(z_out.at[pl.ds(0, n_gx - 1), y_span(h)], xb_send.at[h])
    wait_for(edge_in.at[pl.ds(0, n_gy - 1)], edge_send)
    wait_for(inflow_in.at[pl.ds(0, n_gy - 1)], flow_send)


def per_device(
    forcing_field, innovations, owner_device, column_index, obs_weight, vert_inverse, vert_basis,
    vert_eigen,
):
    n_gx = lax.axis_size("gx")
    n_gy = lax.axis_size("gy")
    devices = n_gx * n_gy
    levels, rows_y, cols_x = forcing_field.shape
    row_total = innovations.shape[0]
    length = cols_x * n_gx
    (c_hi, c_lo), (t_hi, t_lo), line = wave_tables(length)
    own_levels = levels // n_gx
    planes = R_CUTS * R_PLANES
    vmem = pl.BlockSpec(memory_space=pltpu.VMEM)
    smem = pl.BlockSpec(memory_space=pltpu.SMEM)
    hbm = pl.BlockSpec(memory_space=pl.ANY)
    dma = pltpu.SemaphoreType.DMA
    out = pl.pallas_call(
        functools.partial(field_kernel, n_gx, n_gy, (4, 8)),
        out_shape=jax.ShapeDtypeStruct((levels * rows_y, cols_x), F32),
        in_specs=[hbm, vmem, vmem, vmem, vmem, vmem, vmem, smem, hbm, hbm, hbm, hbm, vmem],
        out_specs=vmem,
        scratch_shapes=[
            pltpu.VMEM((levels * rows_y, LANES), F32),
            pltpu.VMEM((length, length), BF16),
            pltpu.VMEM((length, length), BF16),
            pltpu.VMEM((length, length), BF16),
            pltpu.VMEM((length, length), BF16),
            pltpu.VMEM((devices, row_total), BF16),
            pltpu.VMEM((2 * LANES, row_total), BF16),
            pltpu.VMEM((planes, devices, LANES), F32),
            pltpu.VMEM((planes, n_gx, n_gy, LANES), F32),
            pltpu.VMEM((R_CUTS, n_gy, R_PLANES, n_gx, LANES), F32),
            pltpu.VMEM((R_CUTS, n_gy, R_PLANES, n_gx, LANES), F32),
            pltpu.VMEM((8 * levels, rows_y * cols_x // 4), F32),
            pltpu.VMEM((rows_y, levels, LANES), F32),
            pltpu.VMEM((n_gx, rows_y, own_levels, LANES), F32),
            pltpu.VMEM((rows_y, own_levels, length), F32),
            pltpu.VMEM((rows_y, own_levels, length), F32),
            pltpu.VMEM((n_gy, 4, LANES), F32),
            pltpu.VMEM((n_gy, 4, LANES), F32),
            pltpu.VMEM((n_gy, 4, LANES), F32),
            pltpu.VMEM((n_gy, 4, LANES), F32),
            pltpu.VMEM((2, own_levels, length), F32),
            pltpu.VMEM((n_gx, rows_y, own_levels, LANES), F32),
            pltpu.VMEM((rows_y, levels, LANES), F32),
            dma((5,)),
            dma((R_CUTS,)), dma((R_CUTS,)),
            dma((R_CUTS,)), dma((R_CUTS,)),
            dma((Y_CUTS,)), dma((Y_CUTS,)),
            dma(()), dma(()),
            dma(()), dma(()),
            dma((Y_CUTS,)), dma((Y_CUTS,)),
        ],
        compiler_params=pltpu.CompilerParams(
            collective_id=0, has_side_effects=True, vmem_limit_bytes=56 * 1024 * 1024
        ),
        name="field_solve",
    )(
        forcing_field.reshape(levels * rows_y, cols_x), innovations.T,
        owner_device.T, column_index.reshape(1, -1), obs_weight,
        vert_inverse, vert_basis, vert_eigen,
        t_hi, t_lo, c_hi, c_lo, line.reshape(1, -1),
    )
    return out.reshape(levels, rows_y, cols_x)


def solution(mesh):
    return jax.shard_map(
        per_device,
        mesh=mesh,
        in_specs=(
            P(None, "gy", "gx"),
            P(("gx", "gy"), None),
            P(("gx", "gy"), None),
            P(("gx", "gy")),
            P(),
            P(),
            P(),
            P(),
        ),
        out_specs=P(None, "gy", "gx"),
        check_vma=False,
    )
```

time: 132 us -> 96.3 us (0.73)
  Pallas kernels: 121 us -> 93.9 us
  local copies, waits for them, and re-layouts: 8.72 us -> 2.26 us
  other arithmetic: 1.36 us -> 0 us
    pallas_call x1, Pallas kernels: 121 us -> 93.9 us  [per_device(): pl.pallas_call(functools.partial(field_kernel, n_gx, n_gy, (4, 8)), out_s...]
    unnamed x3 -> x1, local copies, waits for them, and re-layouts: 5.12 us -> 2.26 us
    reshape x2 -> x0, local copies, waits for them, and re-layouts: 1.89 us -> none  [the longest x1 1.29 us: per_device(): column_index.reshape(-1, TILE)]
    another operation x1 -> x0, local copies, waits for them, and re-layouts: 1.7 us -> none
    unnamed x1 -> x0, other arithmetic: 1.36 us -> none
where the time goes in v3:
time: 96.3 us; the launch traced here: 96.1 us
  Pallas kernels  93.9 us (98%)
  local copies, waits for them, and re-layouts  2.26 us (2%)
    pallas_call x1, Pallas kernels, per_device(): pl.pallas_call(functools.partial(field_kernel, n_gx, n_gy, (4, 8)), out_s...  93.9 us
    unnamed x1, local copies, waits for them, and re-layouts  2.26 us

profile of v3, /device:TPU:1, one launch (start us, length us, event | category | flops | bytes accessed | tf_op | source)
XLA Modules:
  0.0 96.1 jit_solution(5347844259045790480)
XLA Ops:
  0.0 93.9 %field_solve.1 = f32[2048,128]{1,0:T(8,128)} custom-call(f32[2048,128]{1,0:T(8,128)} %bitcast.6, f32[64,2048]{1,0:T(8,128)} %bitcast.7, s32[1,2048]{1,0:T(1,128)} %bitcast.8, s32[1,2048]{1,0:T(1,128)} %bitcast.9, f32[64,64]{1,0:T(8,128)} %weight.1, f32[64,64]{1,0:T(8,128)} %vinv.1, f32[64,64]{1,0:T(8,128)} %vbas.1, f32[64]{0:T(128)} %eigen.1, ...), custom_call_target="tpu_custom_call" | custom-call | tf_op jit(solution)/shard_map/field_solve/pallas_call | solution.py:443
  93.9 2.3 %copy.15 = f32[64,32,128]{2,1,0:T(8,128)} copy(f32[64,32,128]{2,1,0:T(8,128)} %bitcast.5) | data formatting | bytes 2097152

commit v4 on v3

v4 whole, which is shorter than its diff:
```python
import functools

import jax
import jax.numpy as jnp
import ml_dtypes
import numpy as np
from jax import lax
from jax.experimental import pallas as pl
from jax.experimental.pallas import tpu as pltpu
from jax.sharding import PartitionSpec as P

MESH = pl.DeviceIdType.MESH
F32 = jnp.float32
BF16 = jnp.bfloat16
LANES = 128
TILE = 256
CUTS = 2
SLOTS = 16
QUADS = 4
PAIRS = SLOTS // QUADS


def split_table(table):
    high = table.astype(np.float32).astype(ml_dtypes.bfloat16)
    low = (table - high.astype(np.float64)).astype(np.float32).astype(ml_dtypes.bfloat16)
    return high, low


def wave_tables(length):
    waves = np.arange(length, dtype=np.float64)
    scales = np.where(waves == 0, np.sqrt(1.0 / length), np.sqrt(2.0 / length))
    table = scales[:, None] * np.cos(np.pi * waves[:, None] * (2 * waves + 1) / (2 * length))
    line = 4.0 * np.sin(np.pi * waves / (2.0 * length)) ** 2
    return split_table(table), split_table(table.T), line.astype(np.float32)


def halves(value):
    high = value.astype(BF16)
    low = (value - high.astype(F32)).astype(BF16)
    return high, low


def dot(left, right):
    return jnp.dot(left, right, preferred_element_type=F32)


def dot_nt(left, right):
    return lax.dot_general(left, right, (((1,), (1,)), ((), ())), preferred_element_type=F32)


def wait_for(ref, sem):
    pltpu.make_async_copy(ref, ref, sem).wait()


def power(value, doublings):
    for _ in range(doublings):
        value = value * value
    return value


def decay(sigma):
    root = jnp.sqrt(sigma + 0.25 * sigma * sigma)
    return 1.0 / (1.0 + 0.5 * sigma + root), 0.5 / root


def field_kernel(
    n_gx, n_gy, gy_dims,
    field_hbm, innov, owner, column, weight, vinv, vbas, eigen,
    t_hi_hbm, t_lo_hbm, c_hi_hbm, c_lo_hbm, line,
    out,
    field, t_hi, t_lo, c_hi, c_lo,
    hots, expanded, slots, got, turned, rows_in, codes_out, codes_in, code_lines, codes, hot_x,
    vert, x_in, spec, run, edge_out, edge_in, flow_out, flow_in, z_out, phys,
    load_sem, cy_send, cy_recv, cx_send, cx_recv, ry_send, ry_recv, rx_send, rx_recv,
    xf_send, xf_recv, edge_send, edge_recv, flow_send, flow_recv, xb_send, xb_recv,
):
    gx = lax.axis_index("gx")
    gy = lax.axis_index("gy")
    n_hi, n_lo = gy_dims
    devices = n_gx * n_gy
    levels = vinv.shape[0]
    own = levels // n_gx
    few = own // CUTS
    steps = vert.shape[1]
    rows_y = 2 * steps
    length = t_hi.shape[0]
    chunks = owner.shape[1] // TILE
    tiles = length // LANES

    def iota(shape, axis):
        return lax.broadcasted_iota(jnp.int32, shape, axis)

    def gx_peer(step):
        return lax.rem(gx + step, n_gx)

    def gy_peer(step):
        high = lax.rem(gy // n_lo + step // n_lo, n_hi)
        low = lax.rem(gy + step, n_lo)
        return high * n_lo + low

    loads = [
        pltpu.make_async_copy(source, target, load_sem.at[i])
        for i, (source, target) in enumerate(
            [
                (field_hbm, field), (t_hi_hbm, t_hi), (t_lo_hbm, t_lo), (c_hi_hbm, c_hi),
                (c_lo_hbm, c_lo),
            ]
        )
    ]
    for load in loads:
        load.start()

    barrier = pltpu.get_barrier_semaphore()

    def greet_gx(step, carry):
        pl.semaphore_signal(barrier, inc=1, device_id=(gx_peer(step), gy), device_id_type=MESH)
        return carry

    def greet_gy(step, carry):
        pl.semaphore_signal(barrier, inc=1, device_id=(gx, gy_peer(step)), device_id_type=MESH)
        return carry

    lax.fori_loop(1, n_gy, greet_gy, 0)
    lax.fori_loop(1, n_gx, greet_gx, 0)

    def send_gx(source, target, send_sem, recv_sem):
        pltpu.make_async_copy(source(gx), target, recv_sem).start()

        def one(step, carry):
            peer = gx_peer(step)
            pltpu.make_async_remote_copy(
                src_ref=source(peer), dst_ref=target, send_sem=send_sem, recv_sem=recv_sem,
                device_id=(peer, gy), device_id_type=MESH,
            ).start()
            return carry

        lax.fori_loop(1, n_gx, one, 0)

    def send_gy(source, target, send_sem, recv_sem):
        pltpu.make_async_copy(source(gy), target, recv_sem).start()

        def one(step, carry):
            peer = gy_peer(step)
            pltpu.make_async_remote_copy(
                src_ref=source(peer), dst_ref=target, send_sem=send_sem, recv_sem=recv_sem,
                device_id=(gx, peer), device_id_type=MESH,
            ).start()
            return carry

        lax.fori_loop(1, n_gy, one, 0)

    def exact(left, right, dims):
        return lax.dot_general(
            left, right, (dims, ((), ())), precision=lax.Precision.HIGHEST,
            preferred_element_type=F32,
        )

    side = iota((devices, TILE), 0)

    def lanes_of(chunk):
        return slice(chunk * TILE, (chunk + 1) * TILE)

    def number_rows():
        before = jnp.where(iota((TILE, TILE), 0) < iota((TILE, TILE), 1), 1.0, 0.0).astype(BF16)
        seen = jnp.zeros((devices, 1), F32)
        ranks = []
        for chunk in range(chunks):
            name = owner[:, lanes_of(chunk)]
            peer = lax.rem(name, n_gy) * n_gx + name // n_gy
            hot = jnp.where(side == peer, 1.0, 0.0)
            narrow = hot.astype(BF16)
            hots[:, lanes_of(chunk)] = narrow
            earlier = dot(narrow, before) + seen
            ranks.append(jnp.sum(hot * earlier, axis=0, keepdims=True).astype(jnp.int32))
            seen = seen + jnp.sum(hot, axis=1, keepdims=True)
        return ranks

    def place_codes(ranks):
        lane_side = iota((LANES, TILE), 0)
        gy_side = iota((n_gy, TILE), 0)
        high = jnp.zeros((n_gy, LANES), F32)
        low = jnp.zeros((n_gy, LANES), F32)
        for chunk in range(chunks):
            name = owner[:, lanes_of(chunk)]
            rank = ranks[chunk]
            lane = (rank // QUADS * n_gx + name // n_gy) * QUADS + rank % QUADS
            code = column[:, lanes_of(chunk)] + 1
            here = lane_side == lane
            hot = jnp.where(gy_side == lax.rem(name, n_gy), 1.0, 0.0).astype(BF16)
            high += dot_nt(hot, jnp.where(here, (code >> 6).astype(F32), 0.0).astype(BF16))
            low += dot_nt(hot, jnp.where(here, (code & 63).astype(F32), 0.0).astype(BF16))
        codes_out[:, 0, :] = high * 64.0 + low

    def weigh_rows(ranks, c):
        place = iota((LANES, levels), 0)
        pick = place // (QUADS * few) * own + c * few + place % few
        chosen = jnp.where(iota((LANES, levels), 1) == pick, 1.0, 0.0)
        mixed = exact(vinv[...], weight[...], ((1,), (1,)))
        w_hi, w_lo = halves(exact(chosen, mixed, ((1,), (0,))))
        stack = jnp.concatenate([w_hi, w_hi, w_lo], axis=1)
        quad = iota((LANES, TILE), 0) // few % QUADS
        for chunk in range(chunks):
            hi, lo = halves(innov[:, lanes_of(chunk)])
            rows_m = dot(stack, jnp.concatenate([hi, lo, hi], axis=0))
            hi, lo = halves(jnp.where(quad == ranks[chunk] % QUADS, rows_m, 0.0))
            expanded[:LANES, lanes_of(chunk)] = hi
            expanded[LANES:, lanes_of(chunk)] = lo

    def place_rows(ranks, c, pair):
        total = jnp.zeros((devices, TILE), F32)
        for chunk in range(chunks):
            mask = jnp.where(ranks[chunk] // QUADS == pair, 1.0, 0.0).astype(BF16)
            total += dot_nt(hots[:, lanes_of(chunk)] * mask, expanded[:, lanes_of(chunk)])
        slots[c, pair] = total[:, :LANES] + total[:, LANES:]

    ranks = number_rows()
    place_codes(ranks)
    for c in range(CUTS):
        weigh_rows(ranks, c)
        for pair in range(PAIRS):
            place_rows(ranks, c, pair)
        if c == 0:
            pl.semaphore_wait(barrier, n_gx - 1 + n_gy - 1)
            send_gy(lambda b: codes_out.at[b], codes_in.at[gy], cy_send, cy_recv)
        send_gy(
            lambda b: slots.at[c, :, pl.ds(b * n_gx, n_gx), :],
            got.at[c, gy], ry_send.at[c], ry_recv.at[c],
        )

    width = 2 * levels
    place = iota((width, levels), 0)
    pick = place // (2 * few) % n_gx * own + place // (width // CUTS) * few + place % few
    chosen = jnp.where(iota((width, levels), 1) == pick, 1.0, 0.0)
    upper = (place // few) % 2

    def mix_lines(matrix, read, write):
        m_hi, m_lo = halves(matrix)
        stack = jnp.concatenate([m_hi, m_hi, m_lo], axis=1)
        for j in range(0, steps, 2):
            hi, lo = halves(jnp.concatenate([read(j), read(j + 1)], axis=1))
            mixed = dot(stack, jnp.concatenate([hi, lo, hi], axis=0))
            write(j, mixed[:, :LANES])
            write(j + 1, mixed[:, LANES:])

    def read_field(j):
        return jnp.concatenate(
            [field[pl.ds(half * steps + j, levels, stride=rows_y), :] for half in range(2)], axis=0
        )

    def write_vert(j, value):
        for c in range(CUTS):
            vert[c, j] = value[c * levels : (c + 1) * levels, :]

    into = exact(chosen, vinv[...], ((1,), (0,)))
    into = jnp.concatenate([jnp.where(upper == half, into, 0.0) for half in range(2)], axis=1)
    loads[0].wait()
    mix_lines(into, read_field, write_vert)
    for c in range(CUTS):
        send_gx(
            lambda a: vert.at[c, :, pl.ds(a * own, own), :],
            x_in.at[c, gx], xf_send.at[c], xf_recv.at[c],
        )

    wait_for(codes_in, cy_recv)
    turned_codes = codes_in[:, 0, :].T
    group = n_gx * QUADS
    code_lines[...] = jnp.concatenate(
        [turned_codes[pair * group : (pair + 1) * group, :] for pair in range(PAIRS)], axis=1
    )
    send_gx(lambda a: code_lines, codes.at[gx], cx_send, cx_recv)
    for load in loads[1:]:
        load.wait()
    wait_for(codes, cx_recv)
    wide = QUADS * LANES
    x_side = iota((2 * LANES, wide), 0)

    def slot_codes(a, block):
        return jnp.concatenate(
            [codes[a, pl.ds(block * QUADS + quad, 1), :] for quad in range(QUADS)], axis=1
        ).astype(jnp.int32) - 1

    def mark_x(block, carry):
        for a in range(n_gx):
            code = slot_codes(a, block)
            spot = (code // (steps * LANES)) * LANES + (code & (LANES - 1))
            spot = jnp.where(code < 0, -1, spot)
            hot_x[block, :, a * wide : (a + 1) * wide] = jnp.where(x_side == spot, 1.0, 0.0).astype(
                BF16
            )
        return carry

    lax.fori_loop(0, n_gx, mark_x, 0)

    def turn(c):
        wait_for(got.at[c], ry_recv.at[c])
        lines = got.at[c].reshape(n_gy * PAIRS * n_gx, LANES)
        for block in range(n_gx):
            flat = jnp.concatenate(
                [
                    lines[pl.ds(pair * n_gx + block, n_gy, stride=PAIRS * n_gx), :]
                    for pair in range(PAIRS)
                ],
                axis=0,
            )
            turned[c, :, block] = flat.T.reshape(n_gx, 2, 2 * few, LANES)
        send_gx(lambda a: turned.at[c, a], rows_in.at[c, gx], rx_send.at[c], rx_recv.at[c])

    lower = iota((2 * few, LANES), 0) < few

    def add_rows(c):
        def one(block, carry):
            total = jnp.zeros((steps * 2 * few, 2 * LANES), F32)
            for a in range(n_gx):
                step_of = (slot_codes(a, block) // LANES) & (steps - 1)
                parts = []
                for quad in range(QUADS):
                    data = rows_in[c, a, block, quad // 2]
                    hi = data.astype(BF16).astype(F32)
                    lo = data - hi
                    if quad % 2 == 0:
                        both = jnp.where(lower, hi, pltpu.roll(lo, few, 0))
                    else:
                        both = jnp.where(lower, pltpu.roll(hi, few, 0), lo)
                    at = step_of[:, quad * LANES : (quad + 1) * LANES]
                    parts.append(
                        jnp.concatenate(
                            [jnp.where(at == j, both, 0.0) for j in range(steps)], axis=0
                        ).astype(BF16)
                    )
                total += dot_nt(
                    jnp.concatenate(parts, axis=1), hot_x[block, :, a * wide : (a + 1) * wide]
                )
            for j in range(steps):
                both = total[j * 2 * few : (j + 1) * 2 * few, :]
                both = both + pltpu.roll(both, few, 0)
                x_in[c, block, j] += jnp.where(lower, both[:, :LANES], both[:, LANES:])
            return carry

        lax.fori_loop(0, n_gx, one, 0)

    def times_table(lines, hi_table, lo_table, write):
        hi, lo = halves(lines)
        for block in range(length // TILE):
            cols = pl.ds(block * TILE, TILE)
            write(
                block,
                dot(hi, hi_table[:, cols]) + dot(lo, hi_table[:, cols]) + dot(hi, lo_table[:, cols]),
            )

    def level_sigma(c, waves):
        row = iota((2 * few, waves.shape[1]), 0) % few
        sigma = jnp.broadcast_to(waves, row.shape)
        for i in range(few):
            sigma = sigma + jnp.where(row == i, eigen[gx * own + c * few + i], 0.0)
        return sigma

    first = iota((2 * few, length), 0) < few

    def swap(value):
        return pltpu.roll(value, few, 0)

    def solver(c, tile):
        return (tile + 2 * c) % n_hi * n_lo + tile

    def forward(c):
        lines = jnp.concatenate(
            [x_in[c, a].reshape(steps * 2 * few, LANES) for a in range(n_gx)], axis=1
        )

        def set_spec(block, value):
            spec[c, :, :, block * TILE : (block + 1) * TILE] = value.reshape(steps, 2 * few, TILE)

        times_table(lines, t_hi, t_lo, set_spec)
        ratio, scale = decay(level_sigma(c, line[...]))
        jump = power(ratio, steps.bit_length() - 1)
        ahead = jnp.zeros((2 * few, length), F32)
        for j in range(steps):
            ahead = spec[c, j] + ratio * ahead
            run[c, j] = ahead
        behind = jnp.zeros((2 * few, length), F32)
        for j in reversed(range(steps)):
            behind = ratio * behind
            run[c, j] += behind
            behind = spec[c, j] + behind
        edges = jnp.where(first, behind + jump * swap(behind), ahead + jump * swap(ahead))
        for tile in range(tiles):
            edge_out[c, tile] = edges[:, tile * LANES : (tile + 1) * LANES]
        for tile in range(tiles):
            target = solver(c, tile)

            @pl.when(gy == target)
            def _():
                pltpu.make_async_copy(edge_out.at[c, tile], edge_in.at[c, gy], edge_recv.at[c]).start()

            @pl.when(gy != target)
            def _():
                pltpu.make_async_remote_copy(
                    src_ref=edge_out.at[c, tile], dst_ref=edge_in.at[c, gy],
                    send_sem=edge_send.at[c], recv_sem=edge_recv.at[c],
                    device_id=(gx, target), device_id_type=MESH,
                ).start()

        return ratio, scale, jump, ahead, behind

    def solve_edges(c):
        tile = lax.rem(gy, n_lo)
        mine = gy // n_lo == lax.rem(tile + 2 * c, n_hi)

        @pl.when(mine)
        def _():
            part = pl.ds(pl.multiple_of(tile * LANES, LANES), LANES)
            ratio, _ = decay(level_sigma(c, line[:, part]))
            hop = power(ratio, rows_y.bit_length() - 1)
            across = power(hop, n_gy.bit_length() - 1)
            wait_for(edge_in.at[c], edge_recv.at[c])
            right = jnp.zeros((2 * few, LANES), F32)
            left = jnp.zeros((2 * few, LANES), F32)
            for b in range(n_gy):
                right = edge_in[c, b] + hop * right
                left = edge_in[c, n_gy - 1 - b] + hop * left
            mirror = 1.0 / (1.0 - across * across)
            right, left = (
                (swap(left) + across * right) * mirror, (swap(right) + across * left) * mirror
            )
            for b in range(n_gy):
                flow_out[c, b, few:, :] = right[few:, :]
                flow_out[c, n_gy - 1 - b, :few, :] = left[:few, :]
                right = edge_in[c, b] + hop * right
                left = edge_in[c, n_gy - 1 - b] + hop * left
            send_gy(
                lambda b: flow_out.at[c, b], flow_in.at[c, tile], flow_send.at[c], flow_recv.at[c]
            )

    def backward(c, ratio, scale, jump, ahead, behind):
        wait_for(flow_in.at[c], flow_recv.at[c])
        flow = jnp.concatenate([flow_in[c, tile] for tile in range(tiles)], axis=1)
        ahead, behind = (
            jnp.where(first, swap(flow), jump * flow + swap(ahead)),
            jnp.where(first, jump * flow + swap(behind), swap(flow)),
        )
        for j in range(steps):
            ahead = ratio * ahead
            run[c, j] += ahead
        for j in reversed(range(steps)):
            behind = ratio * behind
            run[c, j] = (run[c, j] + behind) * scale

        def set_lines(block, value):
            for i in range(TILE // LANES):
                z_out[c, block * 2 + i] = value[:, i * LANES : (i + 1) * LANES].reshape(
                    steps, 2 * few, LANES
                )

        times_table(run[c].reshape(steps * 2 * few, length), c_hi, c_lo, set_lines)
        send_gx(
            lambda a: z_out.at[c, a], phys.at[c, :, pl.ds(gx * own, own), :],
            xb_send.at[c], xb_recv.at[c],
        )

    for c in range(CUTS):
        turn(c)
    kept = []
    for c in range(CUTS):
        wait_for(x_in.at[c], xf_recv.at[c])
        wait_for(rows_in.at[c], rx_recv.at[c])
        add_rows(c)
        kept.append(forward(c))
    for c in range(CUTS):
        solve_edges(c)
    for c in range(CUTS):
        backward(c, *kept[c])

    out_of = exact(vbas[...], chosen, ((1,), (1,)))
    half_of = (iota((levels, width), 1) // few) % 2
    out_of = jnp.concatenate([jnp.where(half_of == half, out_of, 0.0) for half in range(2)], axis=0)

    def read_phys(j):
        return jnp.concatenate([phys[c, j] for c in range(CUTS)], axis=0)

    def write_out(j, value):
        for half in range(2):
            out[pl.ds(half * steps + j, levels, stride=rows_y), :] = value[
                half * levels : (half + 1) * levels, :
            ]

    for c in range(CUTS):
        wait_for(phys.at[c], xb_recv.at[c])
    mix_lines(out_of, read_phys, write_out)

    wait_for(codes_in.at[pl.ds(0, n_gy - 1)], cy_send)
    wait_for(codes.at[pl.ds(0, n_gx - 1)], cx_send)
    for c in range(CUTS):
        wait_for(got.at[c, pl.ds(0, n_gy - 1)], ry_send.at[c])
        wait_for(rows_in.at[c, pl.ds(0, n_gx - 1)], rx_send.at[c])
        wait_for(x_in.at[c, pl.ds(0, n_gx - 1)], xf_send.at[c])
        wait_for(z_out.at[c, pl.ds(0, n_gx - 1)], xb_send.at[c])
        mine = gy // n_lo == lax.rem(lax.rem(gy, n_lo) + 2 * c, n_hi)

        @pl.when(mine)
        def _():
            wait_for(edge_out.at[c, pl.ds(0, tiles - 1)], edge_send.at[c])
            wait_for(flow_out.at[c, pl.ds(0, n_gy - 1)], flow_send.at[c])

        @pl.when(jnp.logical_not(mine))
        def _():
            wait_for(edge_out.at[c], edge_send.at[c])


def per_device(
    forcing_field, innovations, owner_device, column_index, obs_weight, vert_inverse, vert_basis,
    vert_eigen,
):
    n_gx = lax.axis_size("gx")
    n_gy = lax.axis_size("gy")
    devices = n_gx * n_gy
    levels, rows_y, cols_x = forcing_field.shape
    row_total = innovations.shape[0]
    length = cols_x * n_gx
    (c_hi, c_lo), (t_hi, t_lo), line = wave_tables(length)
    own = levels // n_gx
    steps = rows_y // 2
    few = own // CUTS
    tiles = length // LANES
    vmem = pl.BlockSpec(memory_space=pltpu.VMEM)
    smem = pl.BlockSpec(memory_space=pltpu.SMEM)
    hbm = pl.BlockSpec(memory_space=pl.ANY)
    dma = pltpu.SemaphoreType.DMA

    def buffer(*shape, dtype=F32):
        return pltpu.VMEM(shape, dtype)

    table = buffer(length, length, dtype=BF16)
    out = pl.pallas_call(
        functools.partial(field_kernel, n_gx, n_gy, (4, 8)),
        out_shape=jax.ShapeDtypeStruct((levels * rows_y, cols_x), F32),
        in_specs=[hbm, vmem, vmem, vmem, vmem, vmem, vmem, smem, hbm, hbm, hbm, hbm, vmem],
        out_specs=vmem,
        scratch_shapes=[
            buffer(levels * rows_y, LANES), table, table, table, table,
            buffer(devices, row_total, dtype=BF16),
            buffer(2 * LANES, row_total, dtype=BF16),
            buffer(CUTS, PAIRS, devices, LANES),
            buffer(CUTS, n_gy, PAIRS, n_gx, LANES),
            buffer(CUTS, n_gx, n_gx, 2, 2 * few, LANES),
            buffer(CUTS, n_gx, n_gx, 2, 2 * few, LANES),
            buffer(n_gy, 1, LANES),
            buffer(n_gy, 1, LANES),
            buffer(n_gx * QUADS, LANES),
            buffer(n_gx, n_gx * QUADS, LANES),
            buffer(n_gx, 2 * LANES, n_gx * QUADS * LANES, dtype=BF16),
            buffer(CUTS, steps, n_gx * 2 * few, LANES),
            buffer(CUTS, n_gx, steps, 2 * few, LANES),
            buffer(CUTS, steps, 2 * few, length),
            buffer(CUTS, steps, 2 * few, length),
            buffer(CUTS, tiles, 2 * few, LANES),
            buffer(CUTS, n_gy, 2 * few, LANES),
            buffer(CUTS, n_gy, 2 * few, LANES),
            buffer(CUTS, tiles, 2 * few, LANES),
            buffer(CUTS, n_gx, steps, 2 * few, LANES),
            buffer(CUTS, steps, n_gx * 2 * few, LANES),
            dma((5,)),
            dma(()), dma(()),
            dma(()), dma(()),
            dma((CUTS,)), dma((CUTS,)),
            dma((CUTS,)), dma((CUTS,)),
            dma((CUTS,)), dma((CUTS,)),
            dma((CUTS,)), dma((CUTS,)),
            dma((CUTS,)), dma((CUTS,)),
            dma((CUTS,)), dma((CUTS,)),
        ],
        compiler_params=pltpu.CompilerParams(
            collective_id=0, has_side_effects=True, vmem_limit_bytes=56 * 1024 * 1024
        ),
        name="field_solve",
    )(
        forcing_field.reshape(levels * rows_y, cols_x), innovations.T,
        owner_device.T, column_index.reshape(1, -1), obs_weight,
        vert_inverse, vert_basis, vert_eigen,
        t_hi, t_lo, c_hi, c_lo, line.reshape(1, -1),
    )
    return out.reshape(levels, rows_y, cols_x)


def solution(mesh):
    return jax.shard_map(
        per_device,
        mesh=mesh,
        in_specs=(
            P(None, "gy", "gx"),
            P(("gx", "gy"), None),
            P(("gx", "gy"), None),
            P(("gx", "gy")),
            P(),
            P(),
            P(),
            P(),
        ),
        out_specs=P(None, "gy", "gx"),
        check_vma=False,
    )
```

time: 96.3 us -> 88.2 us (0.916)
  Pallas kernels: 93.9 us -> 85.8 us
    pallas_call x1, Pallas kernels: 93.9 us -> 85.8 us  [per_device(): pl.pallas_call(functools.partial(field_kernel, n_gx, n_gy, (4, 8)), out_s...]
where the time goes in v4:
time: 88.2 us; the launch traced here: 88 us
  Pallas kernels  85.8 us (97%)
  local copies, waits for them, and re-layouts  2.26 us (3%)
    pallas_call x1, Pallas kernels, per_device(): pl.pallas_call(functools.partial(field_kernel, n_gx, n_gy, (4, 8)), out_s...  85.8 us
    unnamed x1, local copies, waits for them, and re-layouts  2.26 us

profile of v4, /device:TPU:1, one launch (start us, length us, event | category | flops | bytes accessed | tf_op | source)
XLA Modules:
  0.0 88.0 jit_solution(14873477602198637735)
XLA Ops:
  0.0 85.8 %field_solve.1 = f32[2048,128]{1,0:T(8,128)} custom-call(f32[2048,128]{1,0:T(8,128)} %bitcast.6, f32[64,2048]{1,0:T(8,128)} %bitcast.7, s32[1,2048]{1,0:T(1,128)} %bitcast.8, s32[1,2048]{1,0:T(1,128)} %bitcast.9, f32[64,64]{1,0:T(8,128)} %weight.1, f32[64,64]{1,0:T(8,128)} %vinv.1, f32[64,64]{1,0:T(8,128)} %vbas.1, f32[64]{0:T(128)} %eigen.1, ...), custom_call_target="tpu_custom_call" | custom-call | tf_op jit(solution)/shard_map/field_solve/pallas_call | solution.py:533
  85.8 2.3 %copy.15 = f32[64,32,128]{2,1,0:T(8,128)} copy(f32[64,32,128]{2,1,0:T(8,128)} %bitcast.5) | data formatting | bytes 2097152

commit v5 on v4

--- a/solution.py
+++ b/solution.py
@@ -272,21 +272,18 @@
         load.wait()
     wait_for(codes, cx_recv)
     wide = QUADS * LANES
-    x_side = iota((2 * LANES, wide), 0)
-
-    def slot_codes(a, block):
-        return jnp.concatenate(
-            [codes[a, pl.ds(block * QUADS + quad, 1), :] for quad in range(QUADS)], axis=1
-        ).astype(jnp.int32) - 1
-
-    def mark_x(block, carry):
-        for a in range(n_gx):
-            code = slot_codes(a, block)
-            spot = (code // (steps * LANES)) * LANES + (code & (LANES - 1))
-            spot = jnp.where(code < 0, -1, spot)
-            hot_x[block, :, a * wide : (a + 1) * wide] = jnp.where(x_side == spot, 1.0, 0.0).astype(
-                BF16
-            )
+    x_lane = iota((LANES, 2 * LANES), 1).astype(F32)
+
+    def mark_x(a, carry):
+        code = codes[a].astype(jnp.int32) - 1
+        spot = code // (steps * LANES) * LANES + (code & (LANES - 1))
+        spot = jnp.where(code < 0, -1, spot).astype(F32)
+        for row in range(n_gx * QUADS):
+            block, quad = divmod(row, QUADS)
+            down = jnp.broadcast_to(spot[row : row + 1, :], (LANES, LANES)).T
+            down = jnp.concatenate([down, down], axis=1)
+            rows = pl.ds(pl.multiple_of(a * wide + quad * LANES, LANES), LANES)
+            hot_x[block, rows, :] = jnp.where(down == x_lane, 1.0, 0.0).astype(BF16)
         return carry
 
     lax.fori_loop(0, n_gx, mark_x, 0)
@@ -311,7 +308,6 @@
         def one(block, carry):
             total = jnp.zeros((steps * 2 * few, 2 * LANES), F32)
             for a in range(n_gx):
-                step_of = (slot_codes(a, block) // LANES) & (steps - 1)
                 parts = []
                 for quad in range(QUADS):
                     data = rows_in[c, a, block, quad // 2]
@@ -321,14 +317,15 @@
                         both = jnp.where(lower, hi, pltpu.roll(lo, few, 0))
                     else:
                         both = jnp.where(lower, pltpu.roll(hi, few, 0), lo)
-                    at = step_of[:, quad * LANES : (quad + 1) * LANES]
+                    code = codes[a, pl.ds(block * QUADS + quad, 1), :].astype(jnp.int32) - 1
+                    at = jnp.broadcast_to((code // LANES) & (steps - 1), (2 * few, LANES))
                     parts.append(
                         jnp.concatenate(
                             [jnp.where(at == j, both, 0.0) for j in range(steps)], axis=0
                         ).astype(BF16)
                     )
-                total += dot_nt(
-                    jnp.concatenate(parts, axis=1), hot_x[block, :, a * wide : (a + 1) * wide]
+                total += dot(
+                    jnp.concatenate(parts, axis=1), hot_x[block, a * wide : (a + 1) * wide, :]
                 )
             for j in range(steps):
                 both = total[j * 2 * few : (j + 1) * 2 * few, :]
@@ -464,10 +461,12 @@
         wait_for(x_in.at[c], xf_recv.at[c])
         wait_for(rows_in.at[c], rx_recv.at[c])
         add_rows(c)
+        if c > 0:
+            solve_edges(c - 1)
         kept.append(forward(c))
     for c in range(CUTS):
-        solve_edges(c)
-    for c in range(CUTS):
+        if c == CUTS - 1:
+            solve_edges(c)
         backward(c, *kept[c])
 
     out_of = exact(vbas[...], chosen, ((1,), (1,)))
@@ -547,7 +546,7 @@
             buffer(n_gy, 1, LANES),
             buffer(n_gx * QUADS, LANES),
             buffer(n_gx, n_gx * QUADS, LANES),
-            buffer(n_gx, 2 * LANES, n_gx * QUADS * LANES, dtype=BF16),
+            buffer(n_gx, n_gx * QUADS * LANES, 2 * LANES, dtype=BF16),
             buffer(CUTS, steps, n_gx * 2 * few, LANES),
             buffer(CUTS, n_gx, steps, 2 * few, LANES),
             buffer(CUTS, steps, 2 * few, length),

time: 88.2 us -> 83.5 us (0.947)
  Pallas kernels: 85.8 us -> 81.1 us
    pallas_call x1, Pallas kernels: 85.8 us -> 81.1 us  [per_device(): pl.pallas_call(functools.partial(field_kernel, n_gx, n_gy, (4, 8)), out_s...]
where the time goes in v5:
time: 83.5 us; the launch traced here: 83.4 us
  Pallas kernels  81.1 us (97%)
  local copies, waits for them, and re-layouts  2.26 us (3%)
    pallas_call x1, Pallas kernels, per_device(): pl.pallas_call(functools.partial(field_kernel, n_gx, n_gy, (4, 8)), out_s...  81.1 us
    unnamed x1, local copies, waits for them, and re-layouts  2.26 us

profile of v5, /device:TPU:1, one launch (start us, length us, event | category | flops | bytes accessed | tf_op | source)
XLA Modules:
  0.0 83.4 jit_solution(15601534321997715946)
XLA Ops:
  0.0 81.1 %field_solve.1 = f32[2048,128]{1,0:T(8,128)} custom-call(f32[2048,128]{1,0:T(8,128)} %bitcast.6, f32[64,2048]{1,0:T(8,128)} %bitcast.7, s32[1,2048]{1,0:T(1,128)} %bitcast.8, s32[1,2048]{1,0:T(1,128)} %bitcast.9, f32[64,64]{1,0:T(8,128)} %weight.1, f32[64,64]{1,0:T(8,128)} %vinv.1, f32[64,64]{1,0:T(8,128)} %vbas.1, f32[64]{0:T(128)} %eigen.1, ...), custom_call_target="tpu_custom_call" | custom-call | tf_op jit(solution)/shard_map/field_solve/pallas_call | solution.py:532
  81.1 2.3 %copy.15 = f32[64,32,128]{2,1,0:T(8,128)} copy(f32[64,32,128]{2,1,0:T(8,128)} %bitcast.5) | data formatting | bytes 2097152

commit v6 on v5

--- a/solution.py
+++ b/solution.py
@@ -16,6 +16,7 @@
 TILE = 256
 CUTS = 2
 SLOTS = 16
+BLOCK_CUTS = 2
 QUADS = 4
 PAIRS = SLOTS // QUADS
 
@@ -69,7 +70,7 @@
     t_hi_hbm, t_lo_hbm, c_hi_hbm, c_lo_hbm, line,
     out,
     field, t_hi, t_lo, c_hi, c_lo,
-    hots, expanded, slots, got, turned, rows_in, codes_out, codes_in, code_lines, codes, hot_x,
+    masked, expanded, slots, got, turned, rows_in, codes_out, codes_in, code_lines, codes, hot_x,
     vert, x_in, spec, run, edge_out, edge_in, flow_out, flow_in, z_out, phys,
     load_sem, cy_send, cy_recv, cx_send, cx_recv, ry_send, ry_recv, rx_send, rx_recv,
     xf_send, xf_recv, edge_send, edge_recv, flow_send, flow_recv, xb_send, xb_recv,
@@ -169,9 +170,11 @@
             peer = lax.rem(name, n_gy) * n_gx + name // n_gy
             hot = jnp.where(side == peer, 1.0, 0.0)
             narrow = hot.astype(BF16)
-            hots[:, lanes_of(chunk)] = narrow
             earlier = dot(narrow, before) + seen
             ranks.append(jnp.sum(hot * earlier, axis=0, keepdims=True).astype(jnp.int32))
+            for pair in range(PAIRS):
+                mask = jnp.where(ranks[chunk] // QUADS == pair, 1.0, 0.0).astype(BF16)
+                masked[pair, :, lanes_of(chunk)] = narrow * mask
             seen = seen + jnp.sum(hot, axis=1, keepdims=True)
         return ranks
 
@@ -206,19 +209,20 @@
             expanded[:LANES, lanes_of(chunk)] = hi
             expanded[LANES:, lanes_of(chunk)] = lo
 
-    def place_rows(ranks, c, pair):
-        total = jnp.zeros((devices, TILE), F32)
-        for chunk in range(chunks):
-            mask = jnp.where(ranks[chunk] // QUADS == pair, 1.0, 0.0).astype(BF16)
-            total += dot_nt(hots[:, lanes_of(chunk)] * mask, expanded[:, lanes_of(chunk)])
-        slots[c, pair] = total[:, :LANES] + total[:, LANES:]
+    def place_rows(c):
+        for pair in range(0, PAIRS, 2):
+            total = dot_nt(
+                masked[pair : pair + 2].reshape(2 * devices, chunks * TILE), expanded[...]
+            )
+            slots[c, pair : pair + 2] = (total[:, :LANES] + total[:, LANES:]).reshape(
+                2, devices, LANES
+            )
 
     ranks = number_rows()
     place_codes(ranks)
     for c in range(CUTS):
         weigh_rows(ranks, c)
-        for pair in range(PAIRS):
-            place_rows(ranks, c, pair)
+        place_rows(c)
         if c == 0:
             pl.semaphore_wait(barrier, n_gx - 1 + n_gy - 1)
             send_gy(lambda b: codes_out.at[b], codes_in.at[gy], cy_send, cy_recv)
@@ -227,6 +231,13 @@
             got.at[c, gy], ry_send.at[c], ry_recv.at[c],
         )
 
+    wait_for(codes_in, cy_recv)
+    turned_codes = codes_in[:, 0, :].T
+    group = n_gx * QUADS
+    code_lines[...] = jnp.concatenate(
+        [turned_codes[pair * group : (pair + 1) * group, :] for pair in range(PAIRS)], axis=1
+    )
+    send_gx(lambda a: code_lines, codes.at[gx], cx_send, cx_recv)
     width = 2 * levels
     place = iota((width, levels), 0)
     pick = place // (2 * few) % n_gx * own + place // (width // CUTS) * few + place % few
@@ -261,16 +272,27 @@
             x_in.at[c, gx], xf_send.at[c], xf_recv.at[c],
         )
 
-    wait_for(codes_in, cy_recv)
-    turned_codes = codes_in[:, 0, :].T
-    group = n_gx * QUADS
-    code_lines[...] = jnp.concatenate(
-        [turned_codes[pair * group : (pair + 1) * group, :] for pair in range(PAIRS)], axis=1
-    )
-    send_gx(lambda a: code_lines, codes.at[gx], cx_send, cx_recv)
-    for load in loads[1:]:
-        load.wait()
-    wait_for(codes, cx_recv)
+    parts = n_gx // BLOCK_CUTS
+
+    def turn(c):
+        wait_for(got.at[c], ry_recv.at[c])
+        lines = got.at[c].reshape(n_gy * PAIRS * n_gx, LANES)
+        for h in range(BLOCK_CUTS):
+            for block in range(h * parts, (h + 1) * parts):
+                flat = jnp.concatenate(
+                    [
+                        lines[pl.ds(pair * n_gx + block, n_gy, stride=PAIRS * n_gx), :]
+                        for pair in range(PAIRS)
+                    ],
+                    axis=0,
+                )
+                turned[c, :, block] = flat.T.reshape(n_gx, 2, 2 * few, LANES)
+            send_gx(
+                lambda a: turned.at[c, a, pl.ds(h * parts, parts)],
+                rows_in.at[c, gx, pl.ds(h * parts, parts)],
+                rx_send.at[c, h], rx_recv.at[c, h],
+            )
+
     wide = QUADS * LANES
     x_lane = iota((LANES, 2 * LANES), 1).astype(F32)
 
@@ -286,29 +308,21 @@
             hot_x[block, rows, :] = jnp.where(down == x_lane, 1.0, 0.0).astype(BF16)
         return carry
 
+    turn(0)
+    for load in loads[1:]:
+        load.wait()
+    wait_for(codes, cx_recv)
     lax.fori_loop(0, n_gx, mark_x, 0)
-
-    def turn(c):
-        wait_for(got.at[c], ry_recv.at[c])
-        lines = got.at[c].reshape(n_gy * PAIRS * n_gx, LANES)
-        for block in range(n_gx):
-            flat = jnp.concatenate(
-                [
-                    lines[pl.ds(pair * n_gx + block, n_gy, stride=PAIRS * n_gx), :]
-                    for pair in range(PAIRS)
-                ],
-                axis=0,
-            )
-            turned[c, :, block] = flat.T.reshape(n_gx, 2, 2 * few, LANES)
-        send_gx(lambda a: turned.at[c, a], rows_in.at[c, gx], rx_send.at[c], rx_recv.at[c])
+    for c in range(1, CUTS):
+        turn(c)
 
     lower = iota((2 * few, LANES), 0) < few
 
-    def add_rows(c):
+    def add_rows(c, h):
         def one(block, carry):
             total = jnp.zeros((steps * 2 * few, 2 * LANES), F32)
             for a in range(n_gx):
-                parts = []
+                pieces = []
                 for quad in range(QUADS):
                     data = rows_in[c, a, block, quad // 2]
                     hi = data.astype(BF16).astype(F32)
@@ -319,13 +333,13 @@
                         both = jnp.where(lower, pltpu.roll(hi, few, 0), lo)
                     code = codes[a, pl.ds(block * QUADS + quad, 1), :].astype(jnp.int32) - 1
                     at = jnp.broadcast_to((code // LANES) & (steps - 1), (2 * few, LANES))
-                    parts.append(
+                    pieces.append(
                         jnp.concatenate(
                             [jnp.where(at == j, both, 0.0) for j in range(steps)], axis=0
                         ).astype(BF16)
                     )
                 total += dot(
-                    jnp.concatenate(parts, axis=1), hot_x[block, a * wide : (a + 1) * wide, :]
+                    jnp.concatenate(pieces, axis=1), hot_x[block, a * wide : (a + 1) * wide, :]
                 )
             for j in range(steps):
                 both = total[j * 2 * few : (j + 1) * 2 * few, :]
@@ -333,7 +347,7 @@
                 x_in[c, block, j] += jnp.where(lower, both[:, :LANES], both[:, LANES:])
             return carry
 
-        lax.fori_loop(0, n_gx, one, 0)
+        lax.fori_loop(h * parts, (h + 1) * parts, one, 0)
 
     def times_table(lines, hi_table, lo_table, write):
         hi, lo = halves(lines)
@@ -442,25 +456,38 @@
             behind = ratio * behind
             run[c, j] = (run[c, j] + behind) * scale
 
-        def set_lines(block, value):
-            for i in range(TILE // LANES):
-                z_out[c, block * 2 + i] = value[:, i * LANES : (i + 1) * LANES].reshape(
+        hi, lo = halves(run[c].reshape(steps * 2 * few, length))
+        pairs = n_gx // 2
+        for step in range(pairs):
+            pair = lax.rem(gx // 2 + 1 + step, pairs)
+            cols = pl.ds(pl.multiple_of(pair * TILE, TILE), TILE)
+            value = dot(hi, c_hi[:, cols]) + dot(lo, c_hi[:, cols]) + dot(hi, c_lo[:, cols])
+            for i in range(2):
+                z_out[c, pair * 2 + i] = value[:, i * LANES : (i + 1) * LANES].reshape(
                     steps, 2 * few, LANES
                 )
-
-        times_table(run[c].reshape(steps * 2 * few, length), c_hi, c_lo, set_lines)
-        send_gx(
-            lambda a: z_out.at[c, a], phys.at[c, :, pl.ds(gx * own, own), :],
-            xb_send.at[c], xb_recv.at[c],
-        )
-
-    for c in range(CUTS):
-        turn(c)
+            target = phys.at[c, :, pl.ds(gx * own, own), :]
+            if step < pairs - 1:
+                for i in range(2):
+                    peer = pair * 2 + lax.rem(gx + i, 2)
+                    pltpu.make_async_remote_copy(
+                        src_ref=z_out.at[c, peer], dst_ref=target, send_sem=xb_send.at[c],
+                        recv_sem=xb_recv.at[c], device_id=(peer, gy), device_id_type=MESH,
+                    ).start()
+            else:
+                peer = pair * 2 + lax.rem(gx + 1, 2)
+                pltpu.make_async_remote_copy(
+                    src_ref=z_out.at[c, peer], dst_ref=target, send_sem=xb_send.at[c],
+                    recv_sem=xb_recv.at[c], device_id=(peer, gy), device_id_type=MESH,
+                ).start()
+                pltpu.make_async_copy(z_out.at[c, gx], target, xb_recv.at[c]).start()
+
     kept = []
     for c in range(CUTS):
         wait_for(x_in.at[c], xf_recv.at[c])
-        wait_for(rows_in.at[c], rx_recv.at[c])
-        add_rows(c)
+        for h in range(BLOCK_CUTS):
+            wait_for(rows_in.at[c, :, pl.ds(h * parts, parts)], rx_recv.at[c, h])
+            add_rows(c, h)
         if c > 0:
             solve_edges(c - 1)
         kept.append(forward(c))
@@ -490,7 +517,10 @@
     wait_for(codes.at[pl.ds(0, n_gx - 1)], cx_send)
     for c in range(CUTS):
         wait_for(got.at[c, pl.ds(0, n_gy - 1)], ry_send.at[c])
-        wait_for(rows_in.at[c, pl.ds(0, n_gx - 1)], rx_send.at[c])
+        for h in range(BLOCK_CUTS):
+            wait_for(
+                rows_in.at[c, pl.ds(0, n_gx - 1), pl.ds(h * parts, parts)], rx_send.at[c, h]
+            )
         wait_for(x_in.at[c, pl.ds(0, n_gx - 1)], xf_send.at[c])
         wait_for(z_out.at[c, pl.ds(0, n_gx - 1)], xb_send.at[c])
         mine = gy // n_lo == lax.rem(lax.rem(gy, n_lo) + 2 * c, n_hi)
@@ -536,7 +566,7 @@
         out_specs=vmem,
         scratch_shapes=[
             buffer(levels * rows_y, LANES), table, table, table, table,
-            buffer(devices, row_total, dtype=BF16),
+            buffer(PAIRS, devices, row_total, dtype=BF16),
             buffer(2 * LANES, row_total, dtype=BF16),
             buffer(CUTS, PAIRS, devices, LANES),
             buffer(CUTS, n_gy, PAIRS, n_gx, LANES),
@@ -561,7 +591,7 @@
             dma(()), dma(()),
             dma(()), dma(()),
             dma((CUTS,)), dma((CUTS,)),
-            dma((CUTS,)), dma((CUTS,)),
+            dma((CUTS, BLOCK_CUTS)), dma((CUTS, BLOCK_CUTS)),
             dma((CUTS,)), dma((CUTS,)),
             dma((CUTS,)), dma((CUTS,)),
             dma((CUTS,)), dma((CUTS,)),

time: 83.5 us -> 78.4 us (0.939)
  Pallas kernels: 81.1 us -> 76 us
    pallas_call x1, Pallas kernels: 81.1 us -> 76 us  [per_device(): pl.pallas_call(functools.partial(field_kernel, n_gx, n_gy, (4, 8)), out_s...]
where the time goes in v6:
time: 78.4 us; the launch traced here: 78.2 us
  Pallas kernels  76 us (97%)
  local copies, waits for them, and re-layouts  2.26 us (3%)
    pallas_call x1, Pallas kernels, per_device(): pl.pallas_call(functools.partial(field_kernel, n_gx, n_gy, (4, 8)), out_s...  76 us
    unnamed x1, local copies, waits for them, and re-layouts  2.26 us

profile of v6, /device:TPU:1, one launch (start us, length us, event | category | flops | bytes accessed | tf_op | source)
XLA Modules:
  0.0 78.2 jit_solution(16621297311806346523)
XLA Ops:
  0.0 76.0 %field_solve.1 = f32[2048,128]{1,0:T(8,128)} custom-call(f32[2048,128]{1,0:T(8,128)} %bitcast.6, f32[64,2048]{1,0:T(8,128)} %bitcast.7, s32[1,2048]{1,0:T(1,128)} %bitcast.8, s32[1,2048]{1,0:T(1,128)} %bitcast.9, f32[64,64]{1,0:T(8,128)} %weight.1, f32[64,64]{1,0:T(8,128)} %vinv.1, f32[64,64]{1,0:T(8,128)} %vbas.1, f32[64]{0:T(128)} %eigen.1, ...), custom_call_target="tpu_custom_call" | custom-call | tf_op jit(solution)/shard_map/field_solve/pallas_call | solution.py:562
  76.0 2.3 %copy.15 = f32[64,32,128]{2,1,0:T(8,128)} copy(f32[64,32,128]{2,1,0:T(8,128)} %bitcast.5) | data formatting | bytes 2097152

commit v7 on v6

--- a/solution.py
+++ b/solution.py
@@ -16,6 +16,7 @@
 TILE = 256
 CUTS = 2
 SLOTS = 16
+MIX_CUTS = 2
 BLOCK_CUTS = 2
 QUADS = 4
 PAIRS = SLOTS // QUADS
@@ -64,14 +65,58 @@
     return 1.0 / (1.0 + 0.5 * sigma + root), 0.5 / root
 
 
+def exact(left, right, dims):
+    return lax.dot_general(
+        left, right, (dims, ((), ())), precision=lax.Precision.HIGHEST, preferred_element_type=F32
+    )
+
+
+def line_rows(levels, n_gx):
+    own, width = levels // n_gx, 2 * levels
+    few = own // CUTS
+    place = lax.broadcasted_iota(jnp.int32, (width, levels), 0)
+    pick = place // (2 * few) % n_gx * own + place // (width // CUTS) * few + place % few
+    level = lax.broadcasted_iota(jnp.int32, (width, levels), 1)
+    return jnp.where(level == pick, 1.0, 0.0), (place // few) % 2
+
+
+def mix_lines(matrix, steps, read, write):
+    m_hi, m_lo = halves(matrix)
+    stack = jnp.concatenate([m_hi, m_hi, m_lo], axis=1)
+    for j in range(0, steps, 2):
+        hi, lo = halves(jnp.concatenate([read(j), read(j + 1)], axis=1))
+        mixed = dot(stack, jnp.concatenate([hi, lo, hi], axis=0))
+        write(j, mixed[:, :LANES])
+        write(j + 1, mixed[:, LANES:])
+
+
+def level_kernel(n_gx, vbas, phys, out):
+    levels, _, steps, _ = out.shape
+    width = 2 * levels
+    few = levels // n_gx // CUTS
+    chosen, _ = line_rows(levels, n_gx)
+    back = exact(vbas[...], chosen, ((1,), (1,)))
+    half_of = (lax.broadcasted_iota(jnp.int32, (levels, width), 1) // few) % 2
+    back = jnp.concatenate([jnp.where(half_of == half, back, 0.0) for half in range(2)], axis=0)
+
+    def read(j):
+        return jnp.concatenate([phys[c, j] for c in range(CUTS)], axis=0)
+
+    def write(j, value):
+        for half in range(2):
+            out[:, half, j, :] = value[half * levels : (half + 1) * levels, :]
+
+    mix_lines(back, steps, read, write)
+
+
 def field_kernel(
     n_gx, n_gy, gy_dims,
-    field_hbm, innov, owner, column, weight, vinv, vbas, eigen,
+    field_hbm, innov, owner, column, weight, vinv, eigen,
     t_hi_hbm, t_lo_hbm, c_hi_hbm, c_lo_hbm, line,
-    out,
+    phys,
     field, t_hi, t_lo, c_hi, c_lo,
     masked, expanded, slots, got, turned, rows_in, codes_out, codes_in, code_lines, codes, hot_x,
-    vert, x_in, spec, run, edge_out, edge_in, flow_out, flow_in, z_out, phys,
+    vert, x_in, spec, run, edge_out, edge_in, flow_out, flow_in, z_out,
     load_sem, cy_send, cy_recv, cx_send, cx_recv, ry_send, ry_recv, rx_send, rx_recv,
     xf_send, xf_recv, edge_send, edge_recv, flow_send, flow_recv, xb_send, xb_recv,
 ):
@@ -99,6 +144,10 @@
         low = lax.rem(gy + step, n_lo)
         return high * n_lo + low
 
+    def hops(step):
+        return min(step // n_lo, n_hi - step // n_lo) + min(step % n_lo, n_lo - step % n_lo)
+
+    far_first = sorted(range(1, n_gy), key=hops, reverse=True)
     loads = [
         pltpu.make_async_copy(source, target, load_sem.at[i])
         for i, (source, target) in enumerate(
@@ -149,12 +198,6 @@
             return carry
 
         lax.fori_loop(1, n_gy, one, 0)
-
-    def exact(left, right, dims):
-        return lax.dot_general(
-            left, right, (dims, ((), ())), precision=lax.Precision.HIGHEST,
-            preferred_element_type=F32,
-        )
 
     side = iota((devices, TILE), 0)
 
@@ -239,19 +282,7 @@
     )
     send_gx(lambda a: code_lines, codes.at[gx], cx_send, cx_recv)
     width = 2 * levels
-    place = iota((width, levels), 0)
-    pick = place // (2 * few) % n_gx * own + place // (width // CUTS) * few + place % few
-    chosen = jnp.where(iota((width, levels), 1) == pick, 1.0, 0.0)
-    upper = (place // few) % 2
-
-    def mix_lines(matrix, read, write):
-        m_hi, m_lo = halves(matrix)
-        stack = jnp.concatenate([m_hi, m_hi, m_lo], axis=1)
-        for j in range(0, steps, 2):
-            hi, lo = halves(jnp.concatenate([read(j), read(j + 1)], axis=1))
-            mixed = dot(stack, jnp.concatenate([hi, lo, hi], axis=0))
-            write(j, mixed[:, :LANES])
-            write(j + 1, mixed[:, LANES:])
+    chosen, upper = line_rows(levels, n_gx)
 
     def read_field(j):
         return jnp.concatenate(
@@ -265,7 +296,7 @@
     into = exact(chosen, vinv[...], ((1,), (0,)))
     into = jnp.concatenate([jnp.where(upper == half, into, 0.0) for half in range(2)], axis=1)
     loads[0].wait()
-    mix_lines(into, read_field, write_vert)
+    mix_lines(into, steps, read_field, write_vert)
     for c in range(CUTS):
         send_gx(
             lambda a: vert.at[c, :, pl.ds(a * own, own), :],
@@ -438,9 +469,14 @@
                 flow_out[c, n_gy - 1 - b, :few, :] = left[:few, :]
                 right = edge_in[c, b] + hop * right
                 left = edge_in[c, n_gy - 1 - b] + hop * left
-            send_gy(
-                lambda b: flow_out.at[c, b], flow_in.at[c, tile], flow_send.at[c], flow_recv.at[c]
-            )
+            target = flow_in.at[c, tile]
+            pltpu.make_async_copy(flow_out.at[c, gy], target, flow_recv.at[c]).start()
+            for step in far_first:
+                peer = gy_peer(step)
+                pltpu.make_async_remote_copy(
+                    src_ref=flow_out.at[c, peer], dst_ref=target, send_sem=flow_send.at[c],
+                    recv_sem=flow_recv.at[c], device_id=(gx, peer), device_id_type=MESH,
+                ).start()
 
     def backward(c, ratio, scale, jump, ahead, behind):
         wait_for(flow_in.at[c], flow_recv.at[c])
@@ -488,30 +524,14 @@
         for h in range(BLOCK_CUTS):
             wait_for(rows_in.at[c, :, pl.ds(h * parts, parts)], rx_recv.at[c, h])
             add_rows(c, h)
-        if c > 0:
-            solve_edges(c - 1)
         kept.append(forward(c))
     for c in range(CUTS):
-        if c == CUTS - 1:
-            solve_edges(c)
+        solve_edges(c)
+    for c in range(CUTS):
         backward(c, *kept[c])
-
-    out_of = exact(vbas[...], chosen, ((1,), (1,)))
-    half_of = (iota((levels, width), 1) // few) % 2
-    out_of = jnp.concatenate([jnp.where(half_of == half, out_of, 0.0) for half in range(2)], axis=0)
-
-    def read_phys(j):
-        return jnp.concatenate([phys[c, j] for c in range(CUTS)], axis=0)
-
-    def write_out(j, value):
-        for half in range(2):
-            out[pl.ds(half * steps + j, levels, stride=rows_y), :] = value[
-                half * levels : (half + 1) * levels, :
-            ]
 
     for c in range(CUTS):
         wait_for(phys.at[c], xb_recv.at[c])
-    mix_lines(out_of, read_phys, write_out)
 
     wait_for(codes_in.at[pl.ds(0, n_gy - 1)], cy_send)
     wait_for(codes.at[pl.ds(0, n_gx - 1)], cx_send)
@@ -559,11 +579,11 @@
         return pltpu.VMEM(shape, dtype)
 
     table = buffer(length, length, dtype=BF16)
-    out = pl.pallas_call(
+    phys = pl.pallas_call(
         functools.partial(field_kernel, n_gx, n_gy, (4, 8)),
-        out_shape=jax.ShapeDtypeStruct((levels * rows_y, cols_x), F32),
-        in_specs=[hbm, vmem, vmem, vmem, vmem, vmem, vmem, smem, hbm, hbm, hbm, hbm, vmem],
-        out_specs=vmem,
+        out_shape=jax.ShapeDtypeStruct((CUTS, steps, n_gx * 2 * few, LANES), F32),
+        in_specs=[hbm, vmem, vmem, vmem, vmem, vmem, smem, hbm, hbm, hbm, hbm, vmem],
+        out_specs=hbm,
         scratch_shapes=[
             buffer(levels * rows_y, LANES), table, table, table, table,
             buffer(PAIRS, devices, row_total, dtype=BF16),
@@ -586,7 +606,6 @@
             buffer(CUTS, n_gy, 2 * few, LANES),
             buffer(CUTS, tiles, 2 * few, LANES),
             buffer(CUTS, n_gx, steps, 2 * few, LANES),
-            buffer(CUTS, steps, n_gx * 2 * few, LANES),
             dma((5,)),
             dma(()), dma(()),
             dma(()), dma(()),
@@ -604,9 +623,22 @@
     )(
         forcing_field.reshape(levels * rows_y, cols_x), innovations.T,
         owner_device.T, column_index.reshape(1, -1), obs_weight,
-        vert_inverse, vert_basis, vert_eigen,
+        vert_inverse, vert_eigen,
         t_hi, t_lo, c_hi, c_lo, line.reshape(1, -1),
     )
+    part = steps // MIX_CUTS
+    out = pl.pallas_call(
+        functools.partial(level_kernel, n_gx),
+        grid=(MIX_CUTS,),
+        out_shape=jax.ShapeDtypeStruct((levels, 2, steps, cols_x), F32),
+        in_specs=[
+            pl.BlockSpec((levels, levels), lambda i: (0, 0)),
+            pl.BlockSpec((CUTS, part, n_gx * 2 * few, LANES), lambda i: (0, i, 0, 0)),
+        ],
+        out_specs=pl.BlockSpec((levels, 2, part, cols_x), lambda i: (0, 0, i, 0)),
+        compiler_params=pltpu.CompilerParams(vmem_limit_bytes=56 * 1024 * 1024),
+        name="levels_back",
+    )(vert_basis, phys)
     return out.reshape(levels, rows_y, cols_x)
 
 

time: 78.4 us -> 73.4 us (0.936)
  Pallas kernels: 76 us -> 73.3 us
  local copies, waits for them, and re-layouts: 2.26 us -> 0 us
    pallas_call x1, Pallas kernels: 76 us -> 69.9 us  [per_device(): pl.pallas_call(functools.partial(field_kernel, n_gx, n_gy, (4, 8)), out_s...]
    pallas_call x0 -> x1, Pallas kernels: none -> 3.4 us  [per_device(): pl.pallas_call(functools.partial(level_kernel, n_gx), grid=(MIX_CUTS,), o...]
    unnamed x1 -> x0, local copies, waits for them, and re-layouts: 2.26 us -> none
where the time goes in v7:
time: 73.4 us; the launch traced here: 73.3 us
  Pallas kernels  73.3 us (100%)
    pallas_call x1, Pallas kernels, per_device(): pl.pallas_call(functools.partial(field_kernel, n_gx, n_gy, (4, 8)), out_s...  69.9 us
    pallas_call x1, Pallas kernels, per_device(): pl.pallas_call(functools.partial(level_kernel, n_gx), grid=(MIX_CUTS,), o...  3.4 us

profile of v7, /device:TPU:1, one launch (start us, length us, event | category | flops | bytes accessed | tf_op | source)
XLA Modules:
  0.0 73.3 jit_solution(2989056309849080780)
XLA Ops:
  0.0 69.9 %field_solve.1.phys = f32[2,16,64,128]{3,2,1,0:T(8,128)} custom-call(f32[2048,128]{1,0:T(8,128)} %bitcast.5, f32[64,2048]{1,0:T(8,128)} %bitcast.6, s32[1,2048]{1,0:T(1,128)} %bitcast.7, s32[1,2048]{1,0:T(1,128)} %bitcast.8, f32[64,64]{1,0:T(8,128)} %weight.1, f32[64,64]{1,0:T(8,128)} %vinv.1, f32[64]{0:T(128)} %eigen.1, ...), custom_call_target="tpu_custom_call" | custom-call | tf_op jit(solution)/shard_map/field_solve/pallas_call | solution.py:582
  69.9 3.4 %levels_back.1 = f32[64,2,16,128]{3,2,1,0:T(8,128)} custom-call(f32[64,64]{1,0:T(8,128)} %vbas.1, f32[2,16,64,128]{3,2,1,0:T(8,128)} %field_solve.1.phys), custom_call_target="tpu_custom_call" | custom-call | tf_op jit(solution)/shard_map/levels_back/pallas_call | solution.py:630

commit v8 on v7

--- a/solution.py
+++ b/solution.py
@@ -80,9 +80,12 @@
     return jnp.where(level == pick, 1.0, 0.0), (place // few) % 2
 
 
-def mix_lines(matrix, steps, read, write):
+def mix_stack(matrix):
     m_hi, m_lo = halves(matrix)
-    stack = jnp.concatenate([m_hi, m_hi, m_lo], axis=1)
+    return jnp.concatenate([m_hi, m_hi, m_lo], axis=1)
+
+
+def mix_lines(stack, steps, read, write):
     for j in range(0, steps, 2):
         hi, lo = halves(jnp.concatenate([read(j), read(j + 1)], axis=1))
         mixed = dot(stack, jnp.concatenate([hi, lo, hi], axis=0))
@@ -90,14 +93,8 @@
         write(j + 1, mixed[:, LANES:])
 
 
-def level_kernel(n_gx, vbas, phys, out):
+def level_kernel(back, phys, out):
     levels, _, steps, _ = out.shape
-    width = 2 * levels
-    few = levels // n_gx // CUTS
-    chosen, _ = line_rows(levels, n_gx)
-    back = exact(vbas[...], chosen, ((1,), (1,)))
-    half_of = (lax.broadcasted_iota(jnp.int32, (levels, width), 1) // few) % 2
-    back = jnp.concatenate([jnp.where(half_of == half, back, 0.0) for half in range(2)], axis=0)
 
     def read(j):
         return jnp.concatenate([phys[c, j] for c in range(CUTS)], axis=0)
@@ -106,14 +103,14 @@
         for half in range(2):
             out[:, half, j, :] = value[half * levels : (half + 1) * levels, :]
 
-    mix_lines(back, steps, read, write)
+    mix_lines(back[...], steps, read, write)
 
 
 def field_kernel(
     n_gx, n_gy, gy_dims,
-    field_hbm, innov, owner, column, weight, vinv, eigen,
+    field_hbm, innov, owner, column, weight, vinv, vbas, eigen,
     t_hi_hbm, t_lo_hbm, c_hi_hbm, c_lo_hbm, line,
-    phys,
+    phys, back,
     field, t_hi, t_lo, c_hi, c_lo,
     masked, expanded, slots, got, turned, rows_in, codes_out, codes_in, code_lines, codes, hot_x,
     vert, x_in, spec, run, edge_out, edge_in, flow_out, flow_in, z_out,
@@ -162,29 +159,19 @@
 
     barrier = pltpu.get_barrier_semaphore()
 
-    def greet_gx(step, carry):
+    for step in far_first:
+        pl.semaphore_signal(barrier, inc=1, device_id=(gx, gy_peer(step)), device_id_type=MESH)
+    for step in range(1, n_gx):
         pl.semaphore_signal(barrier, inc=1, device_id=(gx_peer(step), gy), device_id_type=MESH)
-        return carry
-
-    def greet_gy(step, carry):
-        pl.semaphore_signal(barrier, inc=1, device_id=(gx, gy_peer(step)), device_id_type=MESH)
-        return carry
-
-    lax.fori_loop(1, n_gy, greet_gy, 0)
-    lax.fori_loop(1, n_gx, greet_gx, 0)
 
     def send_gx(source, target, send_sem, recv_sem):
-        pltpu.make_async_copy(source(gx), target, recv_sem).start()
-
-        def one(step, carry):
-            peer = gx_peer(step)
+        for chip, core in ((2, 0), (2, 1), (1, 0), (3, 0), (1, 1), (3, 1), (0, 1)):
+            peer = lax.rem(gx // 2 + chip, n_gx // 2) * 2 + lax.rem(gx + core, 2)
             pltpu.make_async_remote_copy(
                 src_ref=source(peer), dst_ref=target, send_sem=send_sem, recv_sem=recv_sem,
                 device_id=(peer, gy), device_id_type=MESH,
             ).start()
-            return carry
-
-        lax.fori_loop(1, n_gx, one, 0)
+        pltpu.make_async_copy(source(gx), target, recv_sem).start()
 
     def send_gy(source, target, send_sem, recv_sem):
         pltpu.make_async_copy(source(gy), target, recv_sem).start()
@@ -296,12 +283,18 @@
     into = exact(chosen, vinv[...], ((1,), (0,)))
     into = jnp.concatenate([jnp.where(upper == half, into, 0.0) for half in range(2)], axis=1)
     loads[0].wait()
-    mix_lines(into, steps, read_field, write_vert)
+    mix_lines(mix_stack(into), steps, read_field, write_vert)
     for c in range(CUTS):
         send_gx(
             lambda a: vert.at[c, :, pl.ds(a * own, own), :],
             x_in.at[c, gx], xf_send.at[c], xf_recv.at[c],
         )
+
+    back_to = exact(vbas[...], chosen, ((1,), (1,)))
+    half_of = (iota((levels, width), 1) // few) % 2
+    back[...] = mix_stack(
+        jnp.concatenate([jnp.where(half_of == half, back_to, 0.0) for half in range(2)], axis=0)
+    )
 
     parts = n_gx // BLOCK_CUTS
 
@@ -380,14 +373,15 @@
 
         lax.fori_loop(h * parts, (h + 1) * parts, one, 0)
 
+    def times_columns(both, hi_table, lo_table, cols):
+        count = both.shape[0] // 2
+        value = dot(both, hi_table[:, cols])
+        return value[:count] + value[count:] + dot(both[:count], lo_table[:, cols])
+
     def times_table(lines, hi_table, lo_table, write):
-        hi, lo = halves(lines)
+        both = jnp.concatenate(halves(lines), axis=0)
         for block in range(length // TILE):
-            cols = pl.ds(block * TILE, TILE)
-            write(
-                block,
-                dot(hi, hi_table[:, cols]) + dot(lo, hi_table[:, cols]) + dot(hi, lo_table[:, cols]),
-            )
+            write(block, times_columns(both, hi_table, lo_table, pl.ds(block * TILE, TILE)))
 
     def level_sigma(c, waves):
         row = iota((2 * few, waves.shape[1]), 0) % few
@@ -492,12 +486,12 @@
             behind = ratio * behind
             run[c, j] = (run[c, j] + behind) * scale
 
-        hi, lo = halves(run[c].reshape(steps * 2 * few, length))
+        both = jnp.concatenate(halves(run[c].reshape(steps * 2 * few, length)), axis=0)
         pairs = n_gx // 2
         for step in range(pairs):
             pair = lax.rem(gx // 2 + 1 + step, pairs)
             cols = pl.ds(pl.multiple_of(pair * TILE, TILE), TILE)
-            value = dot(hi, c_hi[:, cols]) + dot(lo, c_hi[:, cols]) + dot(hi, c_lo[:, cols])
+            value = times_columns(both, c_hi, c_lo, cols)
             for i in range(2):
                 z_out[c, pair * 2 + i] = value[:, i * LANES : (i + 1) * LANES].reshape(
                     steps, 2 * few, LANES
@@ -579,11 +573,14 @@
         return pltpu.VMEM(shape, dtype)
 
     table = buffer(length, length, dtype=BF16)
-    phys = pl.pallas_call(
+    phys, back = pl.pallas_call(
         functools.partial(field_kernel, n_gx, n_gy, (4, 8)),
-        out_shape=jax.ShapeDtypeStruct((CUTS, steps, n_gx * 2 * few, LANES), F32),
-        in_specs=[hbm, vmem, vmem, vmem, vmem, vmem, smem, hbm, hbm, hbm, hbm, vmem],
-        out_specs=hbm,
+        out_shape=(
+            jax.ShapeDtypeStruct((CUTS, steps, n_gx * 2 * few, LANES), F32),
+            jax.ShapeDtypeStruct((2 * levels, 6 * levels), BF16),
+        ),
+        in_specs=[hbm, vmem, vmem, vmem, vmem, vmem, vmem, smem, hbm, hbm, hbm, hbm, vmem],
+        out_specs=(hbm, vmem),
         scratch_shapes=[
             buffer(levels * rows_y, LANES), table, table, table, table,
             buffer(PAIRS, devices, row_total, dtype=BF16),
@@ -623,22 +620,22 @@
     )(
         forcing_field.reshape(levels * rows_y, cols_x), innovations.T,
         owner_device.T, column_index.reshape(1, -1), obs_weight,
-        vert_inverse, vert_eigen,
+        vert_inverse, vert_basis, vert_eigen,
         t_hi, t_lo, c_hi, c_lo, line.reshape(1, -1),
     )
     part = steps // MIX_CUTS
     out = pl.pallas_call(
-        functools.partial(level_kernel, n_gx),
+        level_kernel,
         grid=(MIX_CUTS,),
         out_shape=jax.ShapeDtypeStruct((levels, 2, steps, cols_x), F32),
         in_specs=[
-            pl.BlockSpec((levels, levels), lambda i: (0, 0)),
+            pl.BlockSpec((2 * levels, 6 * levels), lambda i: (0, 0)),
             pl.BlockSpec((CUTS, part, n_gx * 2 * few, LANES), lambda i: (0, i, 0, 0)),
         ],
         out_specs=pl.BlockSpec((levels, 2, part, cols_x), lambda i: (0, 0, i, 0)),
         compiler_params=pltpu.CompilerParams(vmem_limit_bytes=56 * 1024 * 1024),
         name="levels_back",
-    )(vert_basis, phys)
+    )(back, phys)
     return out.reshape(levels, rows_y, cols_x)
 
 

time: 73.4 us -> 73.1 us (level)
  no operation moved by 1% of the time
where the time goes in v8:
time: 73.1 us; the launch traced here: 73 us
  Pallas kernels  73 us (100%)
    pallas_call x1, Pallas kernels, per_device(): pl.pallas_call(functools.partial(field_kernel, n_gx, n_gy, (4, 8)), out_s...  70.2 us
    pallas_call x1, Pallas kernels, per_device(): pl.pallas_call(level_kernel, grid=(MIX_CUTS,), out_shape=jax.ShapeDtypeSt...  2.86 us

profile of v8, /device:TPU:1, one launch (start us, length us, event | category | flops | bytes accessed | tf_op | source)
XLA Modules:
  0.0 73.0 jit_solution(1775255578960399016)
XLA Ops:
  0.0 70.2 %field_solve.1 = (f32[2,16,64,128]{3,2,1,0:T(8,128)}, bf16[128,384]{1,0:T(8,128)(2,1)}) custom-call(f32[2048,128]{1,0:T(8,128)} %bitcast.5, f32[64,2048]{1,0:T(8,128)} %bitcast.6, s32[1,2048]{1,0:T(1,128)} %bitcast.7, s32[1,2048]{1,0:T(1,128)} %bitcast.8, f32[64,64]{1,0:T(8,128)} %weight.1, f32[64,64]{1,0:T(8,128)} %vinv.1, f32[64,64]{1,0:T(8,128)} %vbas.1, ...), custom_call_target="tpu_custom_call" | custom-call | tf_op jit(solution)/shard_map/field_solve/pallas_call | solution.py:576
  70.2 2.9 %levels_back.1 = f32[64,2,16,128]{3,2,1,0:T(8,128)} custom-call(bf16[128,384]{1,0:T(8,128)(2,1)} %get-tuple-element.7.back, f32[2,16,64,128]{3,2,1,0:T(8,128)} %get-tuple-element.8.phys), custom_call_target="tpu_custom_call" | custom-call | tf_op jit(solution)/shard_map/levels_back/pallas_call | solution.py:627

commit v9 on v8

--- a/solution.py
+++ b/solution.py
@@ -17,7 +17,7 @@
 CUTS = 2
 SLOTS = 16
 MIX_CUTS = 2
-BLOCK_CUTS = 2
+BLOCK_CUTS = 4
 QUADS = 4
 PAIRS = SLOTS // QUADS
 
@@ -142,7 +142,8 @@
         return high * n_lo + low
 
     def hops(step):
-        return min(step // n_lo, n_hi - step // n_lo) + min(step % n_lo, n_lo - step % n_lo)
+        high, low = step // n_lo, step % n_lo
+        return min(low, n_lo - low), min(high, n_hi - high)
 
     far_first = sorted(range(1, n_gy), key=hops, reverse=True)
     loads = [
@@ -165,26 +166,26 @@
         pl.semaphore_signal(barrier, inc=1, device_id=(gx_peer(step), gy), device_id_type=MESH)
 
     def send_gx(source, target, send_sem, recv_sem):
-        for chip, core in ((2, 0), (2, 1), (1, 0), (3, 0), (1, 1), (3, 1), (0, 1)):
-            peer = lax.rem(gx // 2 + chip, n_gx // 2) * 2 + lax.rem(gx + core, 2)
+        pltpu.make_async_copy(source(gx), target, recv_sem).start()
+
+        def one(step, carry):
+            peer = gx_peer(step)
             pltpu.make_async_remote_copy(
                 src_ref=source(peer), dst_ref=target, send_sem=send_sem, recv_sem=recv_sem,
                 device_id=(peer, gy), device_id_type=MESH,
             ).start()
-        pltpu.make_async_copy(source(gx), target, recv_sem).start()
+            return carry
+
+        lax.fori_loop(1, n_gx, one, 0)
 
     def send_gy(source, target, send_sem, recv_sem):
-        pltpu.make_async_copy(source(gy), target, recv_sem).start()
-
-        def one(step, carry):
+        for step in far_first:
             peer = gy_peer(step)
             pltpu.make_async_remote_copy(
                 src_ref=source(peer), dst_ref=target, send_sem=send_sem, recv_sem=recv_sem,
                 device_id=(gx, peer), device_id_type=MESH,
             ).start()
-            return carry
-
-        lax.fori_loop(1, n_gy, one, 0)
+        pltpu.make_async_copy(source(gy), target, recv_sem).start()
 
     side = iota((devices, TILE), 0)
 
@@ -463,14 +464,9 @@
                 flow_out[c, n_gy - 1 - b, :few, :] = left[:few, :]
                 right = edge_in[c, b] + hop * right
                 left = edge_in[c, n_gy - 1 - b] + hop * left
-            target = flow_in.at[c, tile]
-            pltpu.make_async_copy(flow_out.at[c, gy], target, flow_recv.at[c]).start()
-            for step in far_first:
-                peer = gy_peer(step)
-                pltpu.make_async_remote_copy(
-                    src_ref=flow_out.at[c, peer], dst_ref=target, send_sem=flow_send.at[c],
-                    recv_sem=flow_recv.at[c], device_id=(gx, peer), device_id_type=MESH,
-                ).start()
+            send_gy(
+                lambda b: flow_out.at[c, b], flow_in.at[c, tile], flow_send.at[c], flow_recv.at[c]
+            )
 
     def backward(c, ratio, scale, jump, ahead, behind):
         wait_for(flow_in.at[c], flow_recv.at[c])

time: 73.1 us -> 72 us (0.985)
  Pallas kernels: 73 us -> 71.9 us
    pallas_call x1, Pallas kernels: 70.2 us -> 69 us  [per_device(): pl.pallas_call(functools.partial(field_kernel, n_gx, n_gy, (4, 8)), out_s...]
where the time goes in v9:
time: 72 us; the launch traced here: 71.9 us
  Pallas kernels  71.9 us (100%)
    pallas_call x1, Pallas kernels, per_device(): pl.pallas_call(functools.partial(field_kernel, n_gx, n_gy, (4, 8)), out_s...  69 us
    pallas_call x1, Pallas kernels, per_device(): pl.pallas_call(level_kernel, grid=(MIX_CUTS,), out_shape=jax.ShapeDtypeSt...  2.86 us

profile of v9, /device:TPU:1, one launch (start us, length us, event | category | flops | bytes accessed | tf_op | source)
XLA Modules:
  0.0 71.9 jit_solution(4235123301931694908)
XLA Ops:
  0.0 69.0 %field_solve.1 = (f32[2,16,64,128]{3,2,1,0:T(8,128)}, bf16[128,384]{1,0:T(8,128)(2,1)}) custom-call(f32[2048,128]{1,0:T(8,128)} %bitcast.5, f32[64,2048]{1,0:T(8,128)} %bitcast.6, s32[1,2048]{1,0:T(1,128)} %bitcast.7, s32[1,2048]{1,0:T(1,128)} %bitcast.8, f32[64,64]{1,0:T(8,128)} %weight.1, f32[64,64]{1,0:T(8,128)} %vinv.1, f32[64,64]{1,0:T(8,128)} %vbas.1, ...), custom_call_target="tpu_custom_call" | custom-call | tf_op jit(solution)/shard_map/field_solve/pallas_call | solution.py:572
  69.0 2.9 %levels_back.1 = f32[64,2,16,128]{3,2,1,0:T(8,128)} custom-call(bf16[128,384]{1,0:T(8,128)(2,1)} %get-tuple-element.7.back, f32[2,16,64,128]{3,2,1,0:T(8,128)} %get-tuple-element.8.phys), custom_call_target="tpu_custom_call" | custom-call | tf_op jit(solution)/shard_map/levels_back/pallas_call | solution.py:623

commit v10 on v9

--- a/solution.py
+++ b/solution.py
@@ -379,11 +379,6 @@
         value = dot(both, hi_table[:, cols])
         return value[:count] + value[count:] + dot(both[:count], lo_table[:, cols])
 
-    def times_table(lines, hi_table, lo_table, write):
-        both = jnp.concatenate(halves(lines), axis=0)
-        for block in range(length // TILE):
-            write(block, times_columns(both, hi_table, lo_table, pl.ds(block * TILE, TILE)))
-
     def level_sigma(c, waves):
         row = iota((2 * few, waves.shape[1]), 0) % few
         sigma = jnp.broadcast_to(waves, row.shape)
@@ -404,39 +399,45 @@
             [x_in[c, a].reshape(steps * 2 * few, LANES) for a in range(n_gx)], axis=1
         )
 
-        def set_spec(block, value):
-            spec[c, :, :, block * TILE : (block + 1) * TILE] = value.reshape(steps, 2 * few, TILE)
-
-        times_table(lines, t_hi, t_lo, set_spec)
+        both = jnp.concatenate(halves(lines), axis=0)
         ratio, scale = decay(level_sigma(c, line[...]))
         jump = power(ratio, steps.bit_length() - 1)
-        ahead = jnp.zeros((2 * few, length), F32)
-        for j in range(steps):
-            ahead = spec[c, j] + ratio * ahead
-            run[c, j] = ahead
-        behind = jnp.zeros((2 * few, length), F32)
-        for j in reversed(range(steps)):
-            behind = ratio * behind
-            run[c, j] += behind
-            behind = spec[c, j] + behind
-        edges = jnp.where(first, behind + jump * swap(behind), ahead + jump * swap(ahead))
-        for tile in range(tiles):
-            edge_out[c, tile] = edges[:, tile * LANES : (tile + 1) * LANES]
-        for tile in range(tiles):
-            target = solver(c, tile)
-
-            @pl.when(gy == target)
-            def _():
-                pltpu.make_async_copy(edge_out.at[c, tile], edge_in.at[c, gy], edge_recv.at[c]).start()
-
-            @pl.when(gy != target)
-            def _():
-                pltpu.make_async_remote_copy(
-                    src_ref=edge_out.at[c, tile], dst_ref=edge_in.at[c, gy],
-                    send_sem=edge_send.at[c], recv_sem=edge_recv.at[c],
-                    device_id=(gx, target), device_id_type=MESH,
-                ).start()
-
+        ends = []
+        for block in range(length // TILE):
+            cols = slice(block * TILE, (block + 1) * TILE)
+            rate, skip, low = ratio[:, cols], jump[:, cols], first[:, cols]
+            spec[c, :, :, cols] = times_columns(both, t_hi, t_lo, cols).reshape(
+                steps, 2 * few, TILE
+            )
+            ahead = jnp.zeros((2 * few, TILE), F32)
+            for j in range(steps):
+                ahead = spec[c, j, :, cols] + rate * ahead
+                run[c, j, :, cols] = ahead
+            behind = jnp.zeros((2 * few, TILE), F32)
+            for j in reversed(range(steps)):
+                behind = rate * behind
+                run[c, j, :, cols] += behind
+                behind = spec[c, j, :, cols] + behind
+            ends.append((ahead, behind))
+            edges = jnp.where(low, behind + skip * swap(behind), ahead + skip * swap(ahead))
+            for i in range(TILE // LANES):
+                edge_out[c, block * 2 + i] = edges[:, i * LANES : (i + 1) * LANES]
+            for tile in range(block * 2, block * 2 + 2):
+                target = solver(c, tile)
+
+                @pl.when(gy == target)
+                def _():
+                    pltpu.make_async_copy(edge_out.at[c, tile], edge_in.at[c, gy], edge_recv.at[c]).start()
+
+                @pl.when(gy != target)
+                def _():
+                    pltpu.make_async_remote_copy(
+                        src_ref=edge_out.at[c, tile], dst_ref=edge_in.at[c, gy],
+                        send_sem=edge_send.at[c], recv_sem=edge_recv.at[c],
+                        device_id=(gx, target), device_id_type=MESH,
+                    ).start()
+
+        ahead, behind = (jnp.concatenate(part, axis=1) for part in zip(*ends))
         return ratio, scale, jump, ahead, behind
 
     def solve_edges(c):

time: 72 us -> 74.2 us (1.031)
  Pallas kernels: 71.9 us -> 74.1 us
    pallas_call x1, Pallas kernels: 69 us -> 71.2 us  [per_device(): pl.pallas_call(functools.partial(field_kernel, n_gx, n_gy, (4, 8)), out_s...]
where the time goes in v10:
time: 74.2 us; the launch traced here: 74.1 us
  Pallas kernels  74.1 us (100%)
    pallas_call x1, Pallas kernels, per_device(): pl.pallas_call(functools.partial(field_kernel, n_gx, n_gy, (4, 8)), out_s...  71.2 us
    pallas_call x1, Pallas kernels, per_device(): pl.pallas_call(level_kernel, grid=(MIX_CUTS,), out_shape=jax.ShapeDtypeSt...  2.86 us

profile of v10, /device:TPU:1, one launch (start us, length us, event | category | flops | bytes accessed | tf_op | source)
XLA Modules:
  0.0 74.1 jit_solution(18165938313313235752)
XLA Ops:
  0.0 71.2 %field_solve.1 = (f32[2,16,64,128]{3,2,1,0:T(8,128)}, bf16[128,384]{1,0:T(8,128)(2,1)}) custom-call(f32[2048,128]{1,0:T(8,128)} %bitcast.5, f32[64,2048]{1,0:T(8,128)} %bitcast.6, s32[1,2048]{1,0:T(1,128)} %bitcast.7, s32[1,2048]{1,0:T(1,128)} %bitcast.8, f32[64,64]{1,0:T(8,128)} %weight.1, f32[64,64]{1,0:T(8,128)} %vinv.1, f32[64,64]{1,0:T(8,128)} %vbas.1, ...), custom_call_target="tpu_custom_call" | custom-call | tf_op jit(solution)/shard_map/field_solve/pallas_call | solution.py:573
  71.2 2.9 %levels_back.1 = f32[64,2,16,128]{3,2,1,0:T(8,128)} custom-call(bf16[128,384]{1,0:T(8,128)(2,1)} %get-tuple-element.7.back, f32[2,16,64,128]{3,2,1,0:T(8,128)} %get-tuple-element.8.phys), custom_call_target="tpu_custom_call" | custom-call | tf_op jit(solution)/shard_map/levels_back/pallas_call | solution.py:624
